TPU v7x, 32 devices: a whole 2x2x4 slice. The times are simulated.
32 devices in a mesh: dp: 8 (over y, x, core), tensor: 4 (over z).
Axes of the slice: x: 2, y: 2, z: 4, core: 2. Of those that a mesh axis runs over, the one named last changes fastest.
Arguments:
- tokens: bfloat16 [2, 1024, 1536], P(None, 'dp'), may hold values from -6 to 6
- context: bfloat16 [2, 48, 1024], P(None, 'dp'), may hold values from -6 to 6
- captions: bfloat16 [2, 48, 256, 4096], P(None, 'dp'), may hold values from -6 to 6
- shapes: int32 [2, 48, 2], P(None, 'dp'), may hold values from 0 to 31, as said below
- text_len: int32 [2, 48], P(None, 'dp'), may hold values from 32 to 256, as said below
- w_query: bfloat16 [1536, 1536], P('dp', 'tensor'), may hold values from -0.15625 to 0.15625
- w_key: bfloat16 [1536, 1536], P('dp', 'tensor'), may hold values from -0.15625 to 0.15625
- w_value: bfloat16 [1536, 1536], P('dp', 'tensor'), may hold values from -0.15625 to 0.15625
- w_out: bfloat16 [1536, 1536], P('dp', 'tensor'), may hold values from -0.625 to 0.625
- w_text_key: bfloat16 [4096, 1536], P('dp', 'tensor'), may hold values from -0.09375 to 0.09375
- w_text_value: bfloat16 [4096, 1536], P('dp', 'tensor'), may hold values from -0.09375 to 0.09375
- w_gate: bfloat16 [1536, 4096], P('dp', 'tensor'), may hold values from -0.15625 to 0.15625
- w_up: bfloat16 [1536, 4096], P('dp', 'tensor'), may hold values from -0.15625 to 0.15625
- w_down: bfloat16 [1536, 4096], P('dp', 'tensor'), may hold values from -0.1875 to 0.1875
- w_adaln: bfloat16 [1024, 6144], P('dp', 'tensor'), may hold values from -0.25 to 0.25
- gain_attn: bfloat16 [1536], P('dp'), may hold values from 0.25 to 1.75
- gain_ffn: bfloat16 [1536], P('dp'), may hold values from 0.25 to 1.75
- gain_query: bfloat16 [64, 24], P('dp', 'tensor'), may hold values from 0.25 to 1.75
- gain_key: bfloat16 [64, 24], P('dp', 'tensor'), may hold values from 0.25 to 1.75
- gain_text: bfloat16 [64, 24], P('dp', 'tensor'), may hold values from 0.25 to 1.75
- cross_gate: bfloat16 [24], P('tensor'), may hold values from -1.5 to 1.5
- cotangent: bfloat16 [2, 1024, 1536], P(None, 'dp'), may hold values from -6 to 6
Outputs:
- result: bfloat16 [2, 1024, 1536], P(None, 'dp')
- grad_tokens: bfloat16 [2, 1024, 1536], P(None, 'dp')
- grad_w_query: float32 [1536, 1536], P('dp', 'tensor')
- grad_w_key: float32 [1536, 1536], P('dp', 'tensor')
- grad_w_value: float32 [1536, 1536], P('dp', 'tensor')
- grad_w_out: float32 [1536, 1536], P('dp', 'tensor')
- grad_w_text_key: float32 [4096, 1536], P('dp', 'tensor')
- grad_w_text_value: float32 [4096, 1536], P('dp', 'tensor')
- grad_w_gate: float32 [1536, 4096], P('dp', 'tensor')
- grad_w_up: float32 [1536, 4096], P('dp', 'tensor')
- grad_w_down: float32 [1536, 4096], P('dp', 'tensor')
- grad_w_adaln: float32 [1024, 6144], P('dp', 'tensor')
- grad_gain_attn: float32 [1536], P('dp')
- grad_gain_ffn: float32 [1536], P('dp')
- grad_gain_query: float32 [64, 24], P('dp', 'tensor')
- grad_gain_key: float32 [64, 24], P('dp', 'tensor')
- grad_gain_text: float32 [64, 24], P('dp', 'tensor')
- grad_cross_gate: float32 [24], P('tensor')
Inputs may be any that keep to these rules, and one draw needn't show every extreme that they name: `shapes`: each slot holds an image of rows x (cols + 1) tokens (cols patch columns and one line-end token per row), packed in slot order from the first token of its device's micro-batch rows; an empty slot has rows = cols = 0, otherwise rows is 2 to 4 and cols 7 to 31. The first slot of each device is never empty; the images of one device in one micro-batch take at most 128 tokens, and in each micro-batch one device is filled exactly by one image of 4 rows and 31 columns. `text_len`: in each micro-batch some slot has all 256 caption tokens live.
All inputs are finite; a program needn't handle non-finite values.
Results may differ from a plain program's by a relative error of at most 0.035.
Values may be sent and summed in bfloat16 or wider, within the bound.
A program may use at most 256 MiB of HBM per device.

v0:
```python
import functools

import jax
import jax.numpy as jnp
from jax import lax
from jax.experimental import pallas as pl
from jax.experimental.pallas import tpu as pltpu
from jax.sharding import PartitionSpec as P

HEAD_DIM = 64
DT = 4096
TXT = 256


EPSILON = 1e-06
MASKED = -1e30
ROPE_BASE = 10000.0
STRIP = 16
F32 = jnp.float32
BF16 = jnp.bfloat16


def image_layout(shapes, count):
    height = shapes[:, 0]
    stride_all = shapes[:, 1] + 1
    extent = height * stride_all
    finish = jnp.cumsum(extent)
    begin = finish - extent
    places = jnp.arange(count, dtype=jnp.int32)
    member = (places[:, None] >= begin[None, :]) & (places[:, None] < finish[None, :])
    member_int = member.astype(jnp.int32)
    inside = jnp.sum(member_int, axis=1)
    slot_ids = jnp.arange(shapes.shape[0], dtype=jnp.int32)
    segment = jnp.sum(member_int * slot_ids[None, :], axis=1)
    stride = jnp.sum(member_int * stride_all[None, :], axis=1) + 1 - inside
    offset = places - jnp.sum(member_int * begin[None, :], axis=1)
    return (member.astype(jnp.float32), segment, inside, offset // stride, offset % stride)


def rope_tables(row_pos, col_pos):
    quarter = HEAD_DIM // 4
    freq = ROPE_BASE ** (-jnp.arange(quarter, dtype=jnp.float32) / quarter)
    angles = jnp.stack(
        [
            row_pos.astype(jnp.float32)[:, None] * freq[None, :],
            col_pos.astype(jnp.float32)[:, None] * freq[None, :],
        ],
        axis=1,
    )
    return (jnp.cos(angles), jnp.sin(angles))


def dot_nn(left, right):
    return lax.dot_general(left, right, (((1,), (0,)), ((), ())), preferred_element_type=F32)


def dot_nt(left, right):
    return lax.dot_general(left, right, (((1,), (1,)), ((), ())), preferred_element_type=F32)


def dot_tn(left, right):
    return lax.dot_general(left, right, (((0,), (0,)), ((), ())), preferred_element_type=F32)


def struct(shape, dtype=BF16):
    return jax.ShapeDtypeStruct(shape, dtype)


def run(body, outs, ins, scratch=(), flops=0, traffic=0):
    return pl.pallas_call(
        body,
        out_shape=outs,
        in_specs=[pl.BlockSpec(memory_space=space) for _, space in ins],
        out_specs=[pl.BlockSpec(memory_space=pltpu.VMEM)] * len(outs),
        scratch_shapes=list(scratch),
        compiler_params=pltpu.CompilerParams(vmem_limit_bytes=48 * 2**20),
        cost_estimate=pl.CostEstimate(flops=flops, bytes_accessed=traffic, transcendentals=0),
    )(*[array for array, _ in ins])


def load(source, target, sem):
    copy = pltpu.make_async_copy(source, target, sem)
    copy.start()
    return copy


def wait_all(copies):
    for copy in copies:
        copy.wait()


def token_columns(member, mods, which, target):
    target[...] = dot_nn(member[...], mods[which]).astype(BF16)


def over_strips(rows, step):
    @pl.loop(0, rows // STRIP)
    def _(index):
        step(pl.ds(pl.multiple_of(index * STRIP, STRIP), STRIP))


def head_sum(values, blocks):
    high = values.astype(BF16)
    low = (values - high.astype(F32)).astype(BF16)
    return dot_nn(high, blocks) + dot_nn(low, blocks)


def head_blocks(width):
    row = lax.broadcasted_iota(jnp.int32, (width, width), 0) // HEAD_DIM
    column = lax.broadcasted_iota(jnp.int32, (width, width), 1) // HEAD_DIM
    return jnp.where(row == column, 1.0, 0.0).astype(BF16)


def swap_pairs(values):
    width = values.shape[1]
    quarter = HEAD_DIM // 4
    lane = lax.broadcasted_iota(jnp.int32, values.shape, 1)
    former = lax.rem(lane, 2 * quarter) < quarter
    return jnp.where(
        former, pltpu.roll(values, width - quarter, 1), pltpu.roll(values, quarter, 1)
    )


def head_norm(values, gain, blocks):
    scale = lax.rsqrt(head_sum(values * values, blocks) * (1.0 / HEAD_DIM) + EPSILON)
    return values * scale * gain


def head_norm_back(values, gain, grad, blocks):
    scale = lax.rsqrt(head_sum(values * values, blocks) * (1.0 / HEAD_DIM) + EPSILON)
    normed = values * scale
    grad_gain = jnp.sum(grad * normed, axis=0, keepdims=True)
    inner = grad * gain
    mean = head_sum(inner * normed, blocks) * (1.0 / HEAD_DIM)
    return scale * (inner - normed * mean), grad_gain


def row_scale(values):
    return lax.rsqrt(jnp.mean(values * values, axis=1, keepdims=True) + EPSILON)


MESH = pl.DeviceIdType.MESH
PAIR, ALONG_X, ALONG_Y = 1, 2, 4


def partner(mask):
    rank = lax.axis_index("dp")
    index = rank
    for bit in (1, 2, 4):
        flip = lax.rem(mask // bit, 2)
        index = index + flip * (bit - 2 * bit * lax.rem(rank // bit, 2))
    return index


def announce(masks, shifts, n_tensor):
    barrier = pltpu.get_barrier_semaphore()
    rank = lax.axis_index("tensor")
    for mask in masks:
        pl.semaphore_signal(
            barrier, inc=1, device_id={"dp": partner(mask)}, device_id_type=MESH
        )
    for shift in shifts:
        pl.semaphore_signal(
            barrier,
            inc=1,
            device_id={"tensor": lax.rem(rank + shift, n_tensor)},
            device_id_type=MESH,
        )


def greet(masks, shifts, n_tensor):
    announce(masks, shifts, n_tensor)
    pl.semaphore_wait(pltpu.get_barrier_semaphore(), len(masks) + len(shifts))


def send(source, target, sems, index, device):
    copy = pltpu.make_async_remote_copy(
        src_ref=source,
        dst_ref=target,
        send_sem=sems.at[(0,) + index],
        recv_sem=sems.at[(1,) + index],
        device_id=device,
        device_id_type=MESH,
    )
    copy.start()
    return copy


def gather_kernel(
    n_tensor, shard_tk, shard_tv, shard_qv, shard_ko, context, attn_own, ffn_own, q_own, k_own,
    t_own, w_adaln, captions,
    text_raw, text_key, text_value, qv, ko, cond_act, mods, attn_gain, ffn_gain, q_gain, k_gain, t_gain,
    small, small_all, product, sums, tk, tv, blocks, block, stage, block_sems, stage_sems, own_sems, shard_sems, small_sems, mod_sems, tensor_sems,
):
    rank, tensor_rank = lax.axis_index("dp"), lax.axis_index("tensor")
    masks = range(1, 8)
    shifts = range(1, n_tensor)
    greet(masks, shifts, n_tensor)
    groups = ((shard_tk, tk), (shard_tv, tv), (shard_qv, qv), (shard_ko, ko))

    def rows_of(shard, index, first, size):
        return pl.ds(pl.multiple_of(index * shard.shape[0] + first, 32), size)

    firsts, seconds, pairs, locals_ = {}, {}, {}, []

    def step_1(number):
        shard, whole = groups[number]
        mine = whole.at[rows_of(shard, rank, 0, shard.shape[0])]
        firsts[number] = [
            send(shard, mine, shard_sems, (number, place), {"dp": partner(mask)})
            for place, mask in ((0, ALONG_X), (1, ALONG_Y))
        ]
        pairs[number] = [send(shard, mine, shard_sems, (number, 4), {"dp": partner(PAIR)})]
        local = pltpu.make_async_copy(shard, mine, own_sems.at[number])
        local.start()
        locals_.append(local)

    def step_2(number):
        shard, whole = groups[number]
        size = shard.shape[0]
        half = size // 2
        seconds[number] = []
        for place, mask, onward, start in ((0, ALONG_X, ALONG_Y, half), (1, ALONG_Y, ALONG_X, 0)):
            firsts[number][place].wait_recv()
            part = whole.at[rows_of(shard, partner(mask), start, half)]
            seconds[number].append(
                send(part, part, shard_sems, (number, 2 + place), {"dp": partner(onward)})
            )
            piece = whole.at[rows_of(shard, partner(mask), 0, size)]
            pairs[number].append(
                send(piece, piece, shard_sems, (number, 5 + place), {"dp": partner(PAIR)})
            )

    def step_3(number):
        shard, whole = groups[number]
        half = shard.shape[0] // 2
        for place, start in ((0, half), (1, 0)):
            seconds[number][place].wait_recv()
            part = whole.at[rows_of(shard, partner(ALONG_X + ALONG_Y), start, half)]
            pairs[number].append(
                send(part, part, shard_sems, (number, 7 + place), {"dp": partner(PAIR)})
            )

    def step_4(number):
        for copy in pairs[number]:
            copy.wait_recv()
        locals_[number].wait()

    count = captions.shape[0]

    def fetch(image, slot):
        return pltpu.make_async_copy(captions.at[image], block.at[slot], block_sems.at[slot])

    outputs = (text_raw, text_key, text_value)
    kinds = ((0, 1), (2,))

    def store(image, slot, kind):
        return [
            pltpu.make_async_copy(
                stage.at[slot, index], outputs[index].at[image], stage_sems.at[slot, index]
            )
            for index in kinds[kind]
        ]

    def text_images(low, high, kind):
        @pl.loop(low, high)
        def _(image):
            slot = lax.rem(image, 2)

            @pl.when(image < count - 1)
            def _():
                fetch(image + 1, 1 - slot).start()

            if kind == 0:

                @pl.when(image == count - 1)
                def _():
                    fetch(0, 1 - slot).start()

            fetch(image, slot).wait()

            @pl.when(image >= 2)
            def _():
                wait_all(store(image - 2, slot, kind))

            if kind == 0:
                raw = dot_nn(block[slot], tk[...])
                stage[slot, 0] = raw.astype(BF16)
                stage[slot, 1] = head_norm(raw, t_gain[...], blocks[...]).astype(BF16)
            else:
                stage[slot, 2] = dot_nn(block[slot], tv[...]).astype(BF16)
            for copy in store(image, slot, kind):
                copy.start()

    fetch(0, 0).start()
    step_1(0)
    blocks[...] = head_blocks(tk.shape[1])
    small_copies = []
    images, slots = context.shape[0] * context.shape[1], context.shape[1]
    depth = w_adaln.shape[0]
    gain_size = attn_own.shape[1]
    heads = q_own.shape[1]
    small[...] = jnp.zeros_like(small)
    for index in range(8):
        for first in range(0, images, slots):
            small[index, first : first + slots, :] = context[
                first // slots, :, index * depth : (index + 1) * depth
            ]
        for row, own in ((16, attn_own), (18, ffn_own)):
            for place, first in enumerate(range(0, gain_size, depth)):
                size = min(depth, gain_size - first)
                small[index, row + place : row + place + 1, :size] = own[:, first : first + size]
        for place, own in enumerate((q_own, k_own, t_own)):
            small[index, 24:32, 8 * place : 8 * place + heads] = own[...]
    for mask in masks:
        small_copies.append(
            send(
                small.at[partner(mask)], small_all.at[rank], small_sems, (mask,),
                {"dp": partner(mask)},
            )
        )
    small_all[rank] = small[rank]
    for copy in small_copies:
        copy.wait_recv()
    width = w_adaln.shape[1]
    contexts = small_all[:, 0:16, :].astype(F32).reshape(8 * 16, depth)
    cond_act[...] = jax.nn.silu(contexts).astype(BF16)
    product[...] = dot_nn(cond_act[...], w_adaln[...]).astype(BF16).reshape(8, 16, width)
    mod_copies = [
        send(
            product.at[partner(mask)], sums.at[mask], mod_sems, (mask,), {"dp": partner(mask)}
        )
        for mask in masks
    ]
    step_2(0)
    step_1(1)
    for row, out in ((16, attn_gain), (18, ffn_gain)):
        for index in range(8):
            for place, first in enumerate(range(0, gain_size, depth)):
                size = min(depth, gain_size - first)
                start = index * gain_size + first
                out[:, start : start + size] = small_all[
                    index, row + place : row + place + 1, :size
                ].astype(F32)
    turned = jnp.transpose(small_all[:, 24:32, :].astype(F32).reshape(HEAD_DIM, depth))
    for place, out in enumerate((q_gain, k_gain, t_gain)):
        for head in range(heads):
            out[:, head * HEAD_DIM : (head + 1) * HEAD_DIM] = turned[
                8 * place + head : 8 * place + head + 1, :
            ]
    sums[0] = product[rank]
    for copy in mod_copies:
        copy.wait_recv()
    total = sums[0].astype(F32)
    for mask in masks:
        total = total + sums[mask].astype(F32)
    mods[tensor_rank] = total.astype(BF16)
    tensor_copies = [
        send(
            mods.at[tensor_rank], mods.at[tensor_rank], tensor_sems, (shift,),
            {"tensor": lax.rem(tensor_rank + shift, n_tensor)},
        )
        for shift in shifts
    ]

    step_3(0)
    step_4(0)
    third = count // 3
    text_images(0, third, 0)
    step_2(1)
    step_1(2)
    step_1(3)
    text_images(third, 2 * third, 0)
    step_3(1)
    text_images(2 * third, count, 0)
    step_4(1)
    text_images(0, third, 1)
    step_2(2)
    step_2(3)
    text_images(third, 2 * third, 1)
    text_images(2 * third, count, 1)
    step_3(2)
    step_3(3)
    step_4(2)
    step_4(3)
    for image in (count - 2, count - 1):
        for kind in (0, 1):
            wait_all(store(image, image % 2, kind))
    for copy in tensor_copies:
        copy.wait_recv()
    for number in range(4):
        for copy in firsts[number] + seconds[number] + pairs[number]:
            copy.wait_send()
    for copy in small_copies + mod_copies + tensor_copies:
        copy.wait_send()


ROUTES = ((0, 1, 2, ALONG_X, ALONG_Y), (1, 2, 1, ALONG_Y, ALONG_X))
REDUCE_STRIP = 32


def over_half(half, step):
    @pl.loop(0, half // REDUCE_STRIP)
    def _(index):
        step(pl.multiple_of(index * REDUCE_STRIP, REDUCE_STRIP))


class Reduce:
    def __init__(self, number, read, out, from_pair, out_2, in_2, out_3, in_3, sems):
        self.number, self.read, self.out, self.sems = number, read, out, sems
        self.from_pair, self.out_2, self.in_2, self.out_3, self.in_3 = (
            from_pair, out_2, in_2, out_3, in_3
        )
        self.half = out.shape[0] // 2
        self.copies, self.arriving = [], {}

    def pair_term(self, piece, low):
        there = pl.ds(low, REDUCE_STRIP)
        return self.read(piece, low) + self.from_pair[piece, there, :].astype(F32)

    def move(self, source, target, index, mask):
        return pltpu.make_async_remote_copy(
            src_ref=source,
            dst_ref=target,
            send_sem=self.sems.at[0, self.number, index],
            recv_sem=self.sems.at[1, self.number, index],
            device_id={"dp": partner(mask)},
            device_id_type=MESH,
        )

    def first(self, piece, source):
        return self.move(source, self.from_pair.at[piece], piece, PAIR)

    def second(self, piece, copy):
        copy.wait_recv()
        self.copies.append(copy)
        for side, close, far, first, last in ROUTES:
            if piece not in (close, 3):
                continue
            slot = 1 if piece == 3 else 0

            def step(low):
                self.out_2[side, slot, pl.ds(low, REDUCE_STRIP), :] = self.pair_term(
                    piece, pl.multiple_of(low + side * self.half, REDUCE_STRIP)
                ).astype(BF16)

            over_half(self.half, step)
            moved = self.move(
                self.out_2.at[side, slot], self.in_2.at[side, slot], 4 + 2 * side + slot, first
            )
            moved.start()
            self.arriving[side, slot] = moved
            self.copies.append(moved)

    def third(self):
        for side, close, far, first, last in ROUTES:
            self.arriving[side, 1].wait_recv()

            def step(low):
                here = pl.ds(low, REDUCE_STRIP)
                there = pl.multiple_of(low + side * self.half, REDUCE_STRIP)
                self.out_3[side, here, :] = (
                    self.pair_term(far, there) + self.in_2[side, 1, here, :].astype(F32)
                ).astype(BF16)

            over_half(self.half, step)
            moved = self.move(self.out_3.at[side], self.in_3.at[side], 8 + side, last)
            moved.start()
            self.arriving[side, 2] = moved
            self.copies.append(moved)

    def last(self):
        for side in (0, 1):
            self.arriving[side, 0].wait_recv()
            self.arriving[side, 2].wait_recv()

            def step(low):
                here = pl.ds(low, REDUCE_STRIP)
                there = pl.multiple_of(low + side * self.half, REDUCE_STRIP)
                self.out[pl.ds(there, REDUCE_STRIP), :] = (
                    self.pair_term(0, there)
                    + self.in_2[side, 0, here, :].astype(F32)
                    + self.in_3[side, here, :].astype(F32)
                )

            over_half(self.half, step)
        for copy in self.copies:
            copy.wait_send()


def reduce_scratch(depth, columns):
    half = depth // 2
    return [
        pltpu.VMEM((4, depth, columns), BF16),
        pltpu.VMEM((2, 2, half, columns), BF16),
        pltpu.VMEM((2, 2, half, columns), BF16),
        pltpu.VMEM((2, half, columns), BF16),
        pltpu.VMEM((2, half, columns), BF16),
    ]


def piece_reader(total, size):
    def read(piece, low):
        first = partner(2 * piece) * size + low
        return total[pl.ds(pl.multiple_of(first, 32), REDUCE_STRIP), :].astype(F32)

    return read


def reduce_firsts(reduce, total, size):
    copies = {}
    for piece in (3, 2, 1, 0):
        copies[piece] = reduce.first(piece, piece_of(total, 2 * piece + 1, size))
        copies[piece].start()
    return copies


def piece_of(total, mask, size):
    return total.at[pl.ds(pl.multiple_of(partner(mask) * size, 64), size)]


class TensorSum:
    def __init__(self, number, n_tensor, arrived, sems):
        self.number, self.n_tensor, self.arrived, self.sems = number, n_tensor, arrived, sems
        self.rank = lax.axis_index("tensor")
        self.size = arrived.shape[1]
        self.others = [
            (shift - 1, lax.rem(self.rank + shift, n_tensor)) for shift in range(1, n_tensor)
        ]

    def block(self, index):
        return pl.ds(pl.multiple_of(index * self.size, 16), self.size)

    def scatter(self, partial):
        self.partial = partial
        self.firsts = [
            send(
                partial.at[self.block(other)], self.arrived.at[place], self.sems,
                (2 * self.number, place), {"tensor": other},
            )
            for place, other in self.others
        ]

    def add(self, out, whole):
        for copy in self.firsts:
            copy.wait_recv()

        @pl.loop(0, self.size // STRIP)
        def _(index):
            low = pl.multiple_of(index * STRIP, STRIP)
            there = pl.ds(pl.multiple_of(self.rank * self.size + low, STRIP), STRIP)
            total = self.partial[there, :].astype(F32)
            for place, _ in self.others:
                total = total + self.arrived[place, pl.ds(low, STRIP), :].astype(F32)
            out[there if whole else pl.ds(low, STRIP), :] = total.astype(BF16)

        for copy in self.firsts:
            copy.wait_send()

    def gather(self, out):
        mine = out.at[self.block(self.rank)]
        self.seconds = [
            send(mine, mine, self.sems, (2 * self.number + 1, place), {"tensor": other})
            for place, other in self.others
        ]

    def finish(self):
        for copy in self.seconds:
            copy.wait()


def tensor_kernel(n_tensor, partial, out, arrived, sems):
    greet((), range(1, n_tensor), n_tensor)
    total = TensorSum(0, n_tensor, arrived, sems)
    total.scatter(partial)
    total.add(out, True)
    total.gather(out)
    total.finish()


def emit_kernel(*refs):
    count = (len(refs) - 16) // 3
    sources, refs = refs[: 3 + count], refs[3 + count :]
    outs, refs = refs[: 6 + count], refs[6 + count :]
    held, (turned_key, turned_value, in_sems, sems) = refs[: 3 + count], refs[3 + count :]
    loads = [load(far, here, in_sems.at[i]) for i, (far, here) in enumerate(zip(sources, held))]
    query, key, value, out, text_key, text_value = outs[:6]
    width = query.shape[1]
    copies = []

    def put(here, target):
        copies.append(load(here, target, sems.at[len(copies)]))

    for index in range(3, 3 + count):
        loads[index].wait()
        put(held[index], outs[3 + index])
    for index, first, second in ((0, query, value), (1, key, out)):
        loads[index].wait()
        put(held[index].at[:, :width], first)
        put(held[index].at[:, width:], second)
    loads[2].wait()
    turned_key[...] = jnp.transpose(held[2][:width, :])
    put(turned_key, text_key)
    turned_value[...] = jnp.transpose(held[2][width:, :])
    put(turned_value, text_value)
    wait_all(copies)


def exchange(body, outs, ins, scratch, collective, vmem=48):
    spaces = [space for _, space in outs]
    return pl.pallas_call(
        body,
        out_shape=[shape for shape, _ in outs],
        in_specs=[pl.BlockSpec(memory_space=space) for _, space in ins],
        out_specs=[pl.BlockSpec(memory_space=space) for space in spaces],
        scratch_shapes=scratch,
        compiler_params=pltpu.CompilerParams(
            collective_id=collective, has_side_effects=True, vmem_limit_bytes=vmem * 2**20
        ),
    )(*[array for array, _ in ins])


def project_kernel(
    tokens, member, gain, q_gain, k_gain, cosine, sine, mods, whole_a, whole_b,
    attn_in, query_raw, key_raw, query_rot, key_rot, value, mat_a, mat_b, mod, sems
):
    copies = [load(whole_a, mat_a, sems.at[0]), load(whole_b, mat_b, sems.at[1])]
    width = q_gain.shape[1]
    token_columns(member, mods, 0, mod)
    blocks = head_blocks(width)

    def step(at):
        x = tokens[at, :].astype(F32)
        normed = x * row_scale(x)
        attn_in[at, :] = (normed * gain[...] * (1.0 + mod[at, :].astype(F32))).astype(BF16)

    over_strips(tokens.shape[0], step)
    wait_all(copies)
    query_raw[...] = dot_nn(attn_in[...], mat_a[:, :width])
    key_raw[...] = dot_nn(attn_in[...], mat_b[:, :width])
    value[...] = dot_nn(attn_in[...], mat_a[:, width:]).astype(BF16)
    for raw, head_gain, out in ((query_raw, q_gain, query_rot), (key_raw, k_gain, key_rot)):
        normed = head_norm(raw[...], head_gain[...], blocks)
        out[...] = (normed * cosine[...] + swap_pairs(normed) * sine[...]).astype(BF16)


def text_kernel(
    live, source, captions, gain, whole_k, whole_v,
    text_raw, text_key, text_value, mat_k, mat_v, sems
):
    image = pl.program_id(0)

    @pl.when(image == 0)
    def _():
        wait_all([load(whole_k, mat_k, sems.at[0]), load(whole_v, mat_v, sems.at[1])])

    @pl.when(live[image] > 0)
    def _():
        raw = dot_nn(captions[0], mat_k[...])
        text_raw[0] = raw.astype(BF16)
        text_key[0] = head_norm(raw, gain[...], head_blocks(raw.shape[1])).astype(BF16)
        text_value[0] = dot_nn(captions[0], mat_v[...]).astype(BF16)


def stack_pair(values):
    lane = lax.broadcasted_iota(jnp.int32, (1, 2 * HEAD_DIM), 1)
    first = jnp.where(lane < HEAD_DIM, 1.0, 0.0).astype(values.dtype)
    second = jnp.where(lane < HEAD_DIM, 0.0, 1.0).astype(values.dtype)
    return jnp.concatenate([values * first, values * second], axis=0)


def unstack_pair(values):
    count = values.shape[0] // 2
    lane = lax.broadcasted_iota(jnp.int32, (count, 2 * HEAD_DIM), 1)
    return jnp.where(lane < HEAD_DIM, values[:count], values[count:])


def twice(values):
    return jnp.concatenate([values, values], axis=0)


def softmax(scores, allowed, rows_live):
    scores = jnp.where(allowed, scores, MASKED)
    expo = jnp.where(allowed, jnp.exp(scores - jnp.max(scores, axis=1, keepdims=True)), 0.0)
    total = jnp.sum(expo, axis=1, keepdims=True)
    if rows_live is not None:
        total = jnp.where(rows_live, total, 1.0)
    return expo * (1.0 / total)


def attend_kernel(
    micro, scale, live, text_len, query, key, value, text_key_far, text_value_far,
    self_id, self_row, segment, gate, whole_b, mixed, cross_out, whole,
    mat_b, text_key, text_value, self_out, sem, sems
):
    text_copies = [
        load(text_key_far, text_key, sems.at[0]), load(text_value_far, text_value, sems.at[1])
    ]
    copies = [load(whole_b, mat_b, sem)]
    rows, width = query.shape
    count = rows // micro
    slots = text_key.shape[0] // micro
    heads = width // HEAD_DIM
    cross_out[...] = jnp.zeros_like(cross_out)

    for batch in range(micro):
        at = slice(batch * count, (batch + 1) * count)
        allowed = twice(self_id[at, :]) == self_row[batch : batch + 1, :]
        for first in range(0, width, 2 * HEAD_DIM):
            lanes = slice(first, first + 2 * HEAD_DIM)
            scores = dot_nt(stack_pair(query[at, lanes]), key[at, lanes]) * scale
            probs = softmax(scores, allowed, None).astype(BF16)
            self_out[at, lanes] = unstack_pair(dot_nn(probs, value[at, lanes]))
    wait_all(text_copies)

    @pl.loop(0, micro * slots)
    def _(image):
        @pl.when(live[image] > 0)
        def _():
            at = pl.ds(pl.multiple_of((image // slots) * count, count), count)
            mine = twice(segment[at, :]) == lax.rem(image, slots)
            column = lax.broadcasted_iota(jnp.int32, (2 * count, TXT), 1)
            allowed = mine & (column < text_len[image])
            for first in range(0, width, 2 * HEAD_DIM):
                lanes = slice(first, first + 2 * HEAD_DIM)
                scores = dot_nt(stack_pair(query[at, lanes]), text_key[image, :, lanes]) * scale
                probs = softmax(scores, allowed, mine).astype(BF16)
                cross_out[at, lanes] += unstack_pair(dot_nn(probs, text_value[image, :, lanes]))

    mixed[...] = (self_out[...] + gate[...] * cross_out[...]).astype(BF16)
    wait_all(copies)
    whole[...] = dot_nt(mixed[...], mat_b[:, width:]).astype(BF16)


def feed_kernel(
    tokens, member, gain, cotangent, mods, attn_out, whole_f,
    hidden, ffn_in, inner, grad_gate, grad_up, grad_out, whole,
    mat, mod_1, mod_2, mod_3, sem
):
    copies = [load(whole_f, mat, sem)]
    units = inner.shape[1]
    mat_a, mat_b, mat_c = [mat.at[:, i * units : (i + 1) * units] for i in range(3)]
    token_columns(member, mods, 1, mod_1)
    token_columns(member, mods, 2, mod_2)
    token_columns(member, mods, 3, mod_3)

    def step(at):
        gate_attn = jnp.tanh(mod_1[at, :].astype(F32))
        state = tokens[at, :].astype(F32) + gate_attn * attn_out[at, :].astype(F32)
        hidden[at, :] = state
        normed = state * row_scale(state)
        ffn_in[at, :] = (normed * gain[...] * (1.0 + mod_2[at, :].astype(F32))).astype(BF16)
        gate_ffn = jnp.tanh(mod_3[at, :].astype(F32))
        grad_out[at, :] = (gate_ffn * cotangent[at, :].astype(F32)).astype(BF16)

    rows = tokens.shape[0]
    over_strips(rows, step)
    wait_all(copies)
    chunk = 256
    for first in range(0, units, chunk):
        span = slice(first, first + chunk)
        gate = dot_nn(ffn_in[...], mat_a[:, span])
        up = dot_nn(ffn_in[...], mat_b[:, span])
        grad_inner = dot_nn(grad_out[...], mat_c[:, span])
        turn = jax.nn.sigmoid(gate)
        active = gate * turn
        inner[:, span] = (active * up).astype(BF16)
        grad_up[:, span] = (grad_inner * active).astype(BF16)
        slope = turn * (1.0 + gate * (1.0 - turn))
        grad_gate[:, span] = (grad_inner * up * slope).astype(BF16)
    width = tokens.shape[1]
    for first in range(0, width, 512):
        span = slice(first, first + 512)
        whole[:, span] = (
            dot_nt(grad_gate[...], mat_a[span, :]) + dot_nt(grad_up[...], mat_b[span, :])
        ).astype(BF16)


def feed_grad_kernel(grad_out, inner, ffn_in, grad_gate, grad_up, total):
    units = inner.shape[1]
    step = 256
    for index, (left, right) in enumerate(
        ((ffn_in, grad_gate), (ffn_in, grad_up), (grad_out, inner))
    ):
        for first in range(0, units, step):
            out = slice(index * units + first, index * units + first + step)
            total[:, out] = dot_tn(left[...], right[:, first : first + step]).astype(BF16)


def feed_out_kernel(inner, whole_f, partial, mat, sem):
    units = inner.shape[1]
    copy = load(whole_f.at[:, 2 * units : 3 * units], mat, sem)
    copy.wait()
    for first in range(0, partial.shape[1], 512):
        span = slice(first, first + 512)
        partial[:, span] = dot_nt(inner[...], mat[span, :]).astype(BF16)


def modulate_back(values, gain, shift, grad):
    scale = row_scale(values)
    normed = values * scale
    inner = grad * gain * (1.0 + shift)
    mean = jnp.mean(inner * normed, axis=1, keepdims=True)
    return scale * (inner - normed * mean), grad * normed


def mixed_grad_kernel(
    hidden, member, gain, cotangent, mods, grad_in, whole_b,
    grad_hidden, grad_out, grad_mixed, mat_b, mod_1, mod_2, sem
):
    copies = [load(whole_b, mat_b, sem)]
    token_columns(member, mods, 1, mod_1)
    token_columns(member, mods, 2, mod_2)

    def step(at):
        back, _ = modulate_back(
            hidden[at, :], gain[...], mod_2[at, :].astype(F32), grad_in[at, :].astype(F32)
        )
        total = cotangent[at, :].astype(F32) + back
        grad_hidden[at, :] = total
        grad_out[at, :] = (jnp.tanh(mod_1[at, :].astype(F32)) * total).astype(BF16)

    over_strips(hidden.shape[0], step)
    wait_all(copies)
    width = grad_mixed.shape[1]
    grad_mixed[...] = dot_nn(grad_out[...], mat_b[:, width:])


def feed_exchange_kernel(
    n_tensor, tokens, member, gain, cotangent, mods, attn_out, whole_f, whole_ko,
    hidden, grad_hidden, grad_attn_out, grad_mixed, result_rows, gate_part, ffn_mod, gain_sum, *rest
):
    outs, rest = rest[:3], rest[3:]
    (
        ffn_in, inner, grad_gate, grad_up, grad_out, ffn_part, out_part,
        mat, mod_1, mod_2, mod_3, grad_in, ffn_rows, wide_grad, rows_grad, *rest
    ) = rest
    totals, rest = rest[:3], rest[3:]
    buffers, (arrived_1, arrived_2, sem, mat_sem, sems, tensor_sems) = rest[:15], rest[15:]
    announce((PAIR, ALONG_X, ALONG_Y), range(1, n_tensor), n_tensor)
    feed_kernel(
        tokens, member, gain, cotangent, mods, attn_out, whole_f,
        hidden, ffn_in, inner, grad_gate, grad_up, grad_out, ffn_part,
        mat, mod_1, mod_2, mod_3, sem,
    )
    pl.semaphore_wait(pltpu.get_barrier_semaphore(), 3 + n_tensor - 1)
    sum_in = TensorSum(0, n_tensor, arrived_1, tensor_sems)
    sum_in.scatter(ffn_part)
    size = outs[0].shape[0]
    reduces, firsts = [], []
    for number, (left, right) in enumerate(
        ((ffn_in, grad_gate), (ffn_in, grad_up), (grad_out, inner))
    ):
        total = totals[number]
        for first in range(0, total.shape[1], 256):
            span = slice(first, first + 256)
            total[:, span] = dot_tn(left[...], right[:, span]).astype(BF16)
        reduce = Reduce(
            number, piece_reader(total, size), outs[number],
            *buffers[5 * number : 5 * number + 5], sems,
        )
        reduces.append(reduce)
        firsts.append(reduce_firsts(reduce, total, size))
    units = inner.shape[1]
    for first in range(0, out_part.shape[1], 512):
        span = slice(first, first + 512)
        out_part[:, span] = dot_nt(inner[...], mat[span, 2 * units :]).astype(BF16)
    sum_out = TensorSum(1, n_tensor, arrived_2, tensor_sems)
    for piece in (3, 2, 1, 0):
        for number in range(3):
            reduces[number].second(piece, firsts[number][piece])
    sum_in.add(grad_in, True)
    sum_in.gather(grad_in)
    for reduce in reduces:
        reduce.third()
    sum_in.finish()
    sum_out.scatter(out_part)
    head_width = grad_mixed.shape[1]
    copy = load(whole_ko.at[:, head_width:], mat.at[:, :head_width], mat_sem)

    def step(at):
        back, _ = modulate_back(
            hidden[at, :], gain[...], mod_2[at, :].astype(F32), grad_in[at, :].astype(F32)
        )
        total = cotangent[at, :].astype(F32) + back
        grad_hidden[at, :] = total
        grad_attn_out[at, :] = (jnp.tanh(mod_1[at, :].astype(F32)) * total).astype(BF16)

    over_strips(hidden.shape[0], step)
    copy.wait()
    grad_mixed[...] = dot_nn(grad_attn_out[...], mat[:, :head_width])
    gain_sum[...] = jnp.zeros_like(gain_sum)

    def scale_step(at):
        state = hidden[at, :]
        product = grad_in[at, :].astype(F32) * state * row_scale(state)
        gain_sum[...] += jnp.sum(
            product * (1.0 + mod_2[at, :].astype(F32)), axis=0, keepdims=True
        )
        wide_grad[at, :] = product * gain[...]

    over_strips(hidden.shape[0], scale_step)
    ffn_mod[...] = segment_sum(member[...], wide_grad[...])
    for reduce in reduces:
        reduce.last()
    sum_out.add(ffn_rows, False)
    first = sum_out.rank * sum_out.size

    def row_step(here):
        at = pl.ds(pl.multiple_of(first + here.start, STRIP), STRIP)
        gate = jnp.tanh(mod_3[at, :].astype(F32))
        out = ffn_rows[here, :].astype(F32)
        result_rows[here, :] = (hidden[at, :] + gate * out).astype(BF16)
        rows_grad[here, :] = cotangent[at, :].astype(F32) * out * (1.0 - gate * gate)

    over_strips(sum_out.size, row_step)
    gate_part[...] = segment_sum(member[sum_out.block(sum_out.rank), :], rows_grad[...]).astype(BF16)


def attend_back_kernel(
    micro, scale, live, text_len, grad_mixed, cross_out, query, key, value, text_key_far,
    text_value_far, text_raw_far, query_raw, key_raw, q_gain, k_gain, t_gain, cosine, sine, self_id, self_row, segment,
    gate, grad_query_b, grad_key_b, grad_value_b, grad_text, gain_sums,
    grad_query, grad_key, grad_cross, grad_turned, gain_turned, text_key, text_value, text_raw, sems,
    *held
):
    held, held_sems = held[:-1], held[-1]
    early = (grad_mixed, cross_out, query, key, value, query_raw, key_raw, cosine, sine)
    copies = [load(far, here, held_sems.at[i]) for i, (far, here) in enumerate(zip(early, held))]
    grad_mixed, cross_out, query, key, value, query_raw, key_raw, cosine, sine = held
    text_copies = [
        load(far, here, sems.at[index])
        for index, (far, here) in enumerate(
            ((text_key_far, text_key), (text_value_far, text_value), (text_raw_far, text_raw))
        )
    ]
    rows, width = query.shape
    count = rows // micro
    slots = text_key.shape[0] // micro
    heads = width // HEAD_DIM
    blocks = head_blocks(width)
    wait_all(copies)
    gate_sum = jnp.sum(grad_mixed[...] * cross_out[...], axis=0, keepdims=True)
    gain_sums[...] = jnp.zeros_like(gain_sums)
    gain_sums[3:4, :] = gate_sum * (1.0 - gate[...] * gate[...])
    grad_cross[...] = (gate[...] * grad_mixed[...]).astype(BF16)
    gain_turned[...] = jnp.zeros_like(gain_turned)
    gain_column = jnp.transpose(jnp.broadcast_to(t_gain[...], (8, width)))[:, :1]
    for batch in range(micro):
        at = slice(batch * count, (batch + 1) * count)
        allowed = twice(self_id[at, :]) == self_row[batch : batch + 1, :]
        for first in range(0, width, 2 * HEAD_DIM):
            lanes = slice(first, first + 2 * HEAD_DIM)
            q, k = stack_pair(query[at, lanes]), key[at, lanes]
            grad = stack_pair(grad_mixed[at, lanes].astype(BF16))
            probs = softmax(dot_nt(q, k) * scale, allowed, None)
            grad_probs = dot_nt(grad, value[at, lanes])
            mean = jnp.sum(probs * grad_probs, axis=1, keepdims=True)
            scaled = (probs * (grad_probs - mean) * scale).astype(BF16)
            grad_query[at, lanes] = unstack_pair(dot_nn(scaled, k))
            grad_key[at, lanes] = dot_tn(scaled, q)
            grad_value_b[at, lanes] = dot_tn(probs.astype(BF16), grad).astype(BF16)

    wait_all(text_copies)

    @pl.loop(0, micro * slots)
    def _(image):
        @pl.when(live[image] == 0)
        def _():
            grad_text[:, pl.ds(pl.multiple_of(image * TXT, TXT), TXT)] = jnp.zeros(
                (2 * width, TXT), BF16
            )

        @pl.when(live[image] > 0)
        def _():
            at = pl.ds(pl.multiple_of((image // slots) * count, count), count)
            tokens = pl.ds(pl.multiple_of(image * TXT, TXT), TXT)
            mine = twice(segment[at, :]) == lax.rem(image, slots)
            column = lax.broadcasted_iota(jnp.int32, (2 * count, TXT), 1)
            allowed = mine & (column < text_len[image])
            for first in range(0, width, 2 * HEAD_DIM):
                lanes = slice(first, first + 2 * HEAD_DIM)
                q, k = stack_pair(query[at, lanes]), text_key[image, :, lanes]
                grad = stack_pair(grad_cross[at, lanes])
                probs = softmax(dot_nt(q, k) * scale, allowed, mine)
                grad_probs = dot_nt(grad, text_value[image, :, lanes])
                mean = jnp.sum(probs * grad_probs, axis=1, keepdims=True)
                scaled = (probs * (grad_probs - mean) * scale).astype(BF16)
                grad_query[at, lanes] += unstack_pair(dot_nn(scaled, k))
                grad_turned[lanes, :] = dot_tn(q, scaled)
                grad_text[width + first : width + first + 2 * HEAD_DIM, tokens] = dot_tn(
                    grad, probs.astype(BF16)
                ).astype(BF16)
            by_head = (heads, HEAD_DIM, TXT)
            raw = jnp.transpose(text_raw[image].astype(F32)).reshape(by_head)
            norm = lax.rsqrt(jnp.mean(raw * raw, axis=1, keepdims=True) + EPSILON)
            normed = raw * norm
            upper = grad_turned[...].reshape(by_head)
            gain_turned[...] += (upper * normed).reshape(width, TXT)
            inner = upper * gain_column.reshape(heads, HEAD_DIM, 1)
            mean = jnp.mean(inner * normed, axis=1, keepdims=True)
            back = norm * (inner - normed * mean)
            grad_text[:width, tokens] = back.reshape(width, TXT).astype(BF16)

    for index, (grad, raw, gain, out) in enumerate(
        (
            (grad_query, query_raw, q_gain, grad_query_b),
            (grad_key, key_raw, k_gain, grad_key_b),
        )
    ):
        turned = grad[...] * cosine[...] + swap_pairs(grad[...] * sine[...])
        back, gain_sum = head_norm_back(raw[...], gain[...], turned, blocks)
        out[...] = back.astype(BF16)
        gain_sums[index : index + 1, :] = gain_sum
    text_sums = jnp.sum(gain_turned[...], axis=1, keepdims=True)
    gain_sums[2:3, :] = jnp.transpose(jnp.broadcast_to(text_sums, (width, 128)))[:1, :]


def attn_grad_kernel(
    attn_in, grad_query, grad_key, grad_value, grad_out, mixed, whole_a, whole_b,
    total_a, total_b, whole, mat_a, mat_b, pair, sems
):
    copies = [load(whole_a, mat_a, sems.at[0]), load(whole_b, mat_b, sems.at[1])]
    width = grad_query.shape[1]
    pair[:, :width] = grad_query[...]
    pair[:, width:] = grad_value[...]
    wait_all(copies)
    for first in range(0, whole.shape[1], 512):
        span = slice(first, first + 512)
        whole[:, span] = (
            dot_nt(pair[...], mat_a[span, :]) + dot_nt(grad_key[...], mat_b[span, :width])
        ).astype(BF16)
    for first in range(0, 2 * width, 256):
        span = slice(first, first + 256)
        total_a[:, span] = dot_tn(attn_in[...], pair[:, span]).astype(BF16)
    total_b[:, :width] = dot_tn(attn_in[...], grad_key[...]).astype(BF16)
    total_b[:, width:] = dot_tn(grad_out[...], mixed[...]).astype(BF16)


def last_exchange_kernel(
    n_tensor, captions, grad_text_far, qv_far, ko_far, tokens_far, hidden_far, attn_far, attn_part,
    member, attn_gain, mods, cond_act, gain_sums, result_rows, gate_part, ffn_mod, ffn_gain_sum,
    out_qv, out_ko, out_text, result, grad_tokens, grad_adaln,
    own_attn, own_ffn, own_query, own_key, own_text, own_gate, *rest
):
    buffers, rest = rest[:15], rest[15:]
    (
        text_total, block, grad_in, gate_parts, other_mod, grad_mod, arrived, mod_a, mod_b, work_grad,
        sums, attn_sum, all_mod, all_sums, all_attn, heads_turned,
        block_sems, sems, tensor_sems, small_sems,
        grad_text, total_qv, total_ko, tokens, grad_hidden, attn_out, load_sems,
    ) = rest
    masks = range(1, 8)
    announce(masks, range(1, n_tensor), n_tensor)
    loads = [
        load(far, here, load_sems.at[i])
        for i, (far, here) in enumerate(
            (
                (grad_text_far, grad_text), (qv_far, total_qv), (ko_far, total_ko),
                (tokens_far, tokens), (hidden_far, grad_hidden), (attn_far, attn_out),
            )
        )
    ]
    pl.semaphore_wait(pltpu.get_barrier_semaphore(), 7 + n_tensor - 1)
    sum_in = TensorSum(0, n_tensor, arrived, tensor_sems)
    sum_in.scatter(attn_part)
    head_width = gain_sums.shape[1]
    sums[0:1, :] = ffn_gain_sum[...]
    for row in range(4):
        sums[1:2, row * head_width : (row + 1) * head_width] = gain_sums[row : row + 1, :]
    rank = lax.axis_index("dp")
    copies = [
        send(sums, all_sums.at[mask], small_sems, (1, mask), {"dp": partner(mask)})
        for mask in masks
    ]
    sum_out = TensorSum(1, n_tensor, arrived, tensor_sems)
    result[sum_out.block(sum_out.rank), :] = result_rows[...]
    gate_parts[0] = gate_part[...]
    gate_copies = [
        send(gate_part, gate_parts.at[place + 1], tensor_sems, (2, place), {"tensor": other})
        for place, other in sum_in.others
    ]
    size = out_qv.shape[0]
    depth = out_text.shape[1]
    reduces, firsts = [], []
    for number, (far, total, out) in enumerate(
        ((qv_far, total_qv, out_qv), (ko_far, total_ko, out_ko))
    ):
        reduce = Reduce(
            number, piece_reader(total, size), out, *buffers[5 * number : 5 * number + 5], sems
        )
        reduces.append(reduce)
        firsts.append(reduce_firsts(reduce, far, size))

    def fetch(mask, slot):
        columns = pl.ds(pl.multiple_of(partner(mask) * depth, 128), depth)
        return pltpu.make_async_copy(
            captions.at[:, columns], block.at[slot], block_sems.at[slot]
        )

    def mask_at(place):
        return 7 - 2 * place + 7 * (place // 4)

    fetch(7, 0).start()

    def read_text(piece, low):
        return text_total[2 * piece, pl.ds(low, REDUCE_STRIP), :].astype(F32)

    text = Reduce(2, read_text, out_text, *buffers[10:], sems)

    def work(low, high):
        @pl.loop(low, high)
        def _(place):
            slot = lax.rem(place, 2)
            mask = mask_at(place)

            @pl.when(place < 7)
            def _():
                fetch(mask_at(place + 1), 1 - slot).start()

            fetch(mask, slot).wait()
            for first in range(0, grad_text.shape[0], 256):
                span = slice(first, first + 256)
                text_total[mask, span, :] = dot_nn(grad_text[span, :], block[slot]).astype(BF16)

    wait_all(loads[:3])
    work(0, 2)
    for piece in (3, 2):
        text.first(piece, text_total.at[2 * piece + 1]).start()
    for piece in (3, 2, 1, 0):
        for number in range(2):
            reduces[number].second(piece, firsts[number][piece])
    work(2, 4)
    text_firsts = {}
    for piece in (3, 2, 1, 0):
        text_firsts[piece] = text.first(piece, text_total.at[2 * piece + 1])
    text_firsts[1].start()
    text_firsts[0].start()
    sum_in.add(grad_in, True)
    sum_in.gather(grad_in)
    for reduce in reduces:
        reduce.third()
    work(4, 5)
    text.second(3, text_firsts[3])
    work(5, 6)
    text.second(2, text_firsts[2])
    work(6, 7)
    text.second(1, text_firsts[1])
    work(7, 8)
    text.second(0, text_firsts[0])
    text.third()
    for copy in gate_copies:
        copy.wait()
    gate_mod = gate_parts[0].astype(F32)
    for place, _ in sum_in.others:
        gate_mod = gate_mod + gate_parts[place + 1].astype(F32)
    other_mod[...] = jnp.where(sum_in.rank == 3, gate_mod, ffn_mod[...])
    wait_all(loads[3:])
    sum_in.finish()
    sum_out.gather(result)
    input_kernel(
        tokens, member, attn_gain, grad_hidden, other_mod, mods, grad_in, attn_out,
        grad_tokens, grad_mod, attn_sum, mod_a, mod_b, work_grad,
    )
    for mask in masks:
        device = {"dp": partner(mask)}
        copies.append(send(grad_mod, all_mod.at[rank], small_sems, (0, mask), device))
        copies.append(send(attn_sum, all_attn.at[mask], small_sems, (2, mask), device))
    all_mod[rank] = grad_mod[...]
    for reduce in reduces:
        reduce.last()
    text.last()
    for copy in copies:
        copy.wait_recv()
    added, attn_added = sums[...], attn_sum[...]
    for mask in masks:
        added = added + all_sums[mask]
        attn_added = attn_added + all_attn[mask]
    grad_adaln[...] = dot_tn(cond_act[...], all_mod[...].reshape(8 * 16, all_mod.shape[2]))
    gain_size = own_attn.shape[1]
    for whole, out in ((attn_added, own_attn), (added[0:1, :], own_ffn)):
        out[...] = whole[:, :gain_size]
        for index in range(1, 8):
            part = whole[:, index * gain_size : (index + 1) * gain_size]
            out[...] = jnp.where(rank == index, part, out[...])
    heads = own_query.shape[1]
    for place, out in enumerate((own_query, own_key, own_text)):
        for head in range(heads):
            first = place * head_width + head * HEAD_DIM
            heads_turned[head : head + 1, :HEAD_DIM] = added[1:2, first : first + HEAD_DIM]
        turned = jnp.transpose(heads_turned[...])
        part = out.shape[0]
        out[...] = turned[:part, :heads]
        for index in range(1, 8):
            here = turned[index * part : (index + 1) * part, :heads]
            out[...] = jnp.where(rank == index, here, out[...])
    for head in range(heads):
        first = 3 * head_width + head * HEAD_DIM
        own_gate[:, head : head + 1] = jnp.sum(
            added[1:2, first : first + HEAD_DIM], axis=1, keepdims=True
        )
    for copy in copies:
        copy.wait_send()
    sum_out.finish()


def segment_sum(member, values):
    high = values.astype(BF16)
    rest = values - high.astype(F32)
    middle = rest.astype(BF16)
    low = (rest - middle.astype(F32)).astype(BF16)
    return dot_tn(member, high) + dot_tn(member, middle) + dot_tn(member, low)


def output_kernel(
    hidden, member, gain, cotangent, mods, ffn_out, grad_in,
    result, grad_mod, grad_gain, mod_2, mod_3, grad
):
    token_columns(member, mods, 2, mod_2)
    token_columns(member, mods, 3, mod_3)
    rank = lax.axis_index("tensor")
    grad_gain[...] = jnp.zeros_like(grad_gain)

    def step(at):
        state = hidden[at, :]
        gate = jnp.tanh(mod_3[at, :].astype(F32))
        out = ffn_out[at, :].astype(F32)
        result[at, :] = (state + gate * out).astype(BF16)
        up = grad_in[at, :].astype(F32)
        product = up * state * row_scale(state)
        grad_gain[...] += jnp.sum(
            product * (1.0 + mod_2[at, :].astype(F32)), axis=0, keepdims=True
        )
        grad_gate = cotangent[at, :].astype(F32) * out * (1.0 - gate * gate)
        grad[at, :] = jnp.where(rank == 2, product * gain[...], grad_gate)

    over_strips(hidden.shape[0], step)
    grad_mod[...] = segment_sum(member[...], grad[...])


def input_kernel(
    tokens, member, gain, grad_hidden, other_mod, mods, grad_in, attn_out,
    grad_tokens, grad_mod, grad_gain, mod_0, mod_1, grad
):
    token_columns(member, mods, 0, mod_0)
    token_columns(member, mods, 1, mod_1)
    rank = lax.axis_index("tensor")
    grad_gain[...] = jnp.zeros_like(grad_gain)

    def step(at):
        shift = mod_0[at, :].astype(F32)
        upper = grad_hidden[at, :]
        back, product = modulate_back(
            tokens[at, :].astype(F32), gain[...], shift, grad_in[at, :].astype(F32)
        )
        grad_tokens[at, :] = (upper + back).astype(BF16)
        grad_gain[...] += jnp.sum(product * (1.0 + shift), axis=0, keepdims=True)
        gate = jnp.tanh(mod_1[at, :].astype(F32))
        grad_gate = upper * attn_out[at, :].astype(F32) * (1.0 - gate * gate)
        grad[at, :] = jnp.where(rank == 0, product * gain[...], grad_gate)

    over_strips(tokens.shape[0], step)
    own = segment_sum(member[...], grad[...])
    grad_mod[...] = jnp.where(rank < 2, own, other_mod[...]).astype(BF16)


def shards(
    n_dp,
    n_tensor,
    tokens,
    context,
    captions,
    shapes,
    text_len,
    w_query,
    w_key,
    w_value,
    w_out,
    w_text_key,
    w_text_value,
    w_gate,
    w_up,
    w_down,
    w_adaln,
    gain_attn,
    gain_ffn,
    gain_query,
    gain_key,
    gain_text,
    cross_gate,
    cotangent,
):
    parts = 8 if n_dp == 8 else 1
    micro, count, width = tokens.shape
    slots = shapes.shape[1]
    rows = micro * count
    images = micro * slots
    heads = w_query.shape[1] // HEAD_DIM
    local = heads * HEAD_DIM
    units = w_gate.shape[1]
    scale = HEAD_DIM ** (-0.5)
    dp_rank = lax.axis_index("dp")
    padded = 16
    vmem, smem, anywhere = pltpu.VMEM, pltpu.SMEM, pl.ANY
    dma = pltpu.SemaphoreType.DMA

    def inside(*arrays):
        return [(array, vmem) for array in arrays]

    def scalars(*arrays):
        return [(array, smem) for array in arrays]

    def outside(*arrays):
        return [(array, anywhere) for array in arrays]

    def after(values, earlier):
        return lax.optimization_barrier((list(values), list(earlier)))[0]

    def gathered(shard):
        return lax.all_gather(shard, "dp", axis=0, tiled=True)

    def scattered(whole):
        return lax.psum_scatter(whole, "dp", scatter_dimension=0, tiled=True).astype(F32)

    part_rows = rows // n_tensor
    arrived = vmem((n_tensor - 1, part_rows, width), BF16)

    def tensor_sum(partial):
        (out,) = exchange(
            functools.partial(tensor_kernel, n_tensor),
            [(struct((rows, width)), vmem)],
            inside(partial),
            [arrived, dma((2, 2, n_tensor - 1))],
            1,
        )
        return out

    gain_list = (gain_attn, gain_ffn, gain_query, gain_key, gain_text)
    cond_rows, span = w_adaln.shape
    shard_qv = jnp.concatenate([w_query, w_value], axis=1)
    shard_ko = jnp.concatenate([w_key, w_out], axis=1)
    shard_f = jnp.concatenate([w_gate, w_up, w_down], axis=1)
    if parts == 1:
        whole_tk, whole_tv = gathered(w_text_key), gathered(w_text_value)
        whole_qv, whole_ko = gathered(shard_qv), gathered(shard_ko)
        gains = [lax.all_gather(gain.astype(F32), "dp", axis=0, tiled=True) for gain in gain_list]
        attn_gain, ffn_gain = [gain.reshape(1, width) for gain in gains[:2]]
        query_gain, key_gain, text_gain = [gain.T.reshape(1, local) for gain in gains[2:]]
        context_all = gathered(context.reshape(images, -1))
        cond_cols = lax.dynamic_slice_in_dim(context_all, dp_rank * cond_rows, cond_rows, 1)
        cond_act = jax.nn.silu(cond_cols.astype(F32)).astype(BF16)
        mod_part = scattered(dot_nn(cond_act, w_adaln)).astype(BF16)
        mods = lax.all_gather(mod_part, "tensor", axis=0)
        mods = jnp.pad(mods, ((0, 0), (0, padded - images), (0, 0)))
    else:
        text_raw, text_key, text_value, whole_qv, whole_ko, cond_act, mods, *gains = exchange(
            functools.partial(gather_kernel, n_tensor),
            [(struct((images, TXT, local)), anywhere)] * 3
            + [(struct((width, 2 * local)), anywhere)] * 2
            + [
                (struct((parts * padded, cond_rows)), vmem),
                (struct((n_tensor, padded, span)), vmem),
            ]
            + [(struct((1, width), F32), vmem)] * 2
            + [(struct((1, local), F32), vmem)] * 3,
            outside(w_text_key, w_text_value, shard_qv, shard_ko)
            + inside(
                context, gain_attn[None], gain_ffn[None], gain_query, gain_key, gain_text, w_adaln
            )
            + outside(captions.reshape(images, TXT, DT)),
            [
                vmem((parts, 2 * padded, cond_rows), BF16),
                vmem((parts, 2 * padded, cond_rows), BF16),
                vmem((parts, padded, span), BF16),
                vmem((parts, padded, span), BF16),
                vmem((DT, local), BF16),
                vmem((DT, local), BF16),
                vmem((local, local), BF16),
                vmem((2, TXT, DT), BF16),
                vmem((2, 3, TXT, local), BF16),
                dma((2,)),
                dma((2, 3)),
                dma((4,)),
                dma((2, 4, 9)),
                dma((2, 8)),
                dma((2, 8)),
                dma((2, n_tensor)),
            ],
            2,
        )
        attn_gain, ffn_gain, query_gain, key_gain, text_gain = gains
        (shard_f,) = after([shard_f], [mods])
    whole_f = gathered(shard_f)
    layouts = [image_layout(shapes[i], count) for i in range(micro)]
    member, segment, inside_any, row_pos, col_pos = [
        jnp.stack([layout[j] for layout in layouts]) for j in range(5)
    ]
    cosine, sine = rope_tables(row_pos.reshape(rows), col_pos.reshape(rows))
    cosine = jnp.tile(jnp.stack([cosine, cosine], axis=2).reshape(rows, HEAD_DIM), (1, heads))
    sine = jnp.tile(jnp.stack([-sine, sine], axis=2).reshape(rows, HEAD_DIM), (1, heads))
    which = jnp.arange(micro, dtype=jnp.int32)
    member = jnp.where(
        (which[:, None] == which[None, :])[:, None, :, None], member[:, :, None, :], 0.0
    )
    member = jnp.pad(member.reshape(rows, images), ((0, 0), (0, padded - images))).astype(BF16)
    self_row = jnp.where(inside_any > 0, segment, slots)
    self_id = self_row.reshape(rows, 1)
    segment = segment.reshape(rows, 1)
    lens = text_len.reshape(images)
    used = shapes[:, :, 0] * (shapes[:, :, 1] + 1) > 0
    used = used | (jnp.arange(slots)[None, :] == 0)
    live = used.reshape(images).astype(jnp.int32)
    at = jnp.arange(images, dtype=jnp.int32)
    source = lax.cummax(jnp.where(live > 0, at, 0))
    gate = jnp.repeat(jnp.tanh(cross_gate.astype(F32)), HEAD_DIM)[None, :]
    token_rows = tokens.reshape(rows, width)
    grad_y = cotangent.reshape(rows, width)
    caption_images = captions.reshape(images, TXT, DT)

    attn_in, query_raw, key_raw, query_rot, key_rot, value = run(
        project_kernel,
        [struct((rows, width))]
        + [struct((rows, local), F32)] * 2
        + [struct((rows, local))] * 3,
        inside(token_rows, member, attn_gain, query_gain, key_gain, cosine, sine, mods)
        + outside(whole_qv, whole_ko),
        [
            vmem((width, 2 * local), BF16),
            vmem((width, 2 * local), BF16),
            vmem((rows, width), BF16),
            dma((2,)),
        ],
        flops=6 * rows * width * local,
        traffic=10 * 2**20,
    )

    if parts == 1:
        text_raw, text_key, text_value = pl.pallas_call(
            text_kernel,
            out_shape=[struct((images, TXT, local))] * 3,
            grid_spec=pltpu.PrefetchScalarGridSpec(
                num_scalar_prefetch=2,
                grid=(images,),
                in_specs=[
                    pl.BlockSpec((1, TXT, DT), lambda i, live, source: (source[i], 0, 0)),
                    pl.BlockSpec((1, local), lambda i, live, source: (0, 0)),
                ]
                + [pl.BlockSpec(memory_space=anywhere)] * 2,
                out_specs=[pl.BlockSpec((1, TXT, local), lambda i, live, source: (i, 0, 0))] * 3,
                scratch_shapes=[vmem((DT, local), BF16), vmem((DT, local), BF16), dma((2,))],
            ),
            compiler_params=pltpu.CompilerParams(vmem_limit_bytes=40 * 2**20),
            cost_estimate=pl.CostEstimate(
                flops=2 * images * TXT * DT * local, bytes_accessed=20 * 2**20, transcendentals=0
            ),
        )(live, source, caption_images, text_gain, whole_tk, whole_tv)

    wide = vmem((rows, width), BF16)
    mixed, cross_out, attn_part = run(
        functools.partial(attend_kernel, micro, scale),
        [struct((rows, local)), struct((rows, local), F32), struct((rows, width))],
        scalars(live, lens)
        + inside(query_rot, key_rot, value)
        + outside(text_key, text_value)
        + inside(self_id, self_row, segment, gate)
        + outside(whole_ko),
        [
            vmem((width, 2 * local), BF16),
            vmem((images, TXT, local), BF16),
            vmem((images, TXT, local), BF16),
            vmem((rows, local), F32),
            dma,
            dma((2,)),
        ],
        flops=2 * 2**30,
        traffic=12 * 2**20,
    )
    attn_out = tensor_sum(attn_part)

    size = width // parts
    if parts == 1:
        mat = vmem((width, 3 * units), BF16)
        hidden, ffn_in, inner, grad_gate, grad_up, grad_ffn_out, ffn_part = run(
            feed_kernel,
            [struct((rows, width), F32), struct((rows, width))]
            + [struct((rows, units))] * 3
            + [struct((rows, width))] * 2,
            inside(token_rows, member, ffn_gain, grad_y, mods, attn_out) + outside(whole_f),
            [mat, wide, wide, wide, dma],
            flops=10 * rows * width * units,
            traffic=20 * 2**20,
        )
        (grad_f,) = run(
            feed_grad_kernel,
            [struct((width, 3 * units))],
            inside(grad_ffn_out, inner, ffn_in, grad_gate, grad_up),
            flops=6 * rows * width * units,
            traffic=12 * 2**20,
        )
        (ffn_part,) = after([ffn_part], [grad_f])
        grad_ffn_in = tensor_sum(ffn_part)
        grad_f = scattered(grad_f)
        (ffn_out_part,) = run(
            feed_out_kernel,
            [struct((rows, width))],
            inside(inner) + outside(whole_f),
            [vmem((width, units), BF16), dma],
            flops=2 * rows * width * units,
            traffic=5 * 2**20,
        )
        ffn_out = lax.psum(ffn_out_part, "tensor")

        grad_hidden, grad_attn_out, grad_mixed = run(
            mixed_grad_kernel,
            [struct((rows, width), F32), struct((rows, width)), struct((rows, local), F32)],
            inside(hidden, member, ffn_gain, grad_y, mods, grad_ffn_in) + outside(whole_ko),
            [vmem((width, 2 * local), BF16), wide, wide, dma],
            flops=2 * rows * width * local,
            traffic=8 * 2**20,
        )
    else:
        (
            hidden, grad_hidden, grad_attn_out, grad_mixed, result_rows, gate_part, ffn_mod,
            ffn_gain_sum, *grad_f
        ) = exchange(
            functools.partial(feed_exchange_kernel, n_tensor),
            [
                (struct((rows, width), F32), vmem),
                (struct((rows, width), F32), vmem),
                (struct((rows, width)), vmem),
                (struct((rows, local), F32), vmem),
                (struct((part_rows, width)), vmem),
                (struct((padded, width)), vmem),
                (struct((padded, width), F32), vmem),
                (struct((1, width), F32), vmem),
            ]
            + [(struct((size, units), F32), vmem)] * 3,
            inside(token_rows, member, ffn_gain, grad_y, mods, attn_out)
            + outside(whole_f, whole_ko),
            [wide]
            + [vmem((rows, units), BF16)] * 3
            + [wide] * 3
            + [vmem((width, 3 * units), BF16), wide, wide, wide, wide]
            + [
                vmem((part_rows, width), BF16),
                vmem((rows, width), F32),
                vmem((part_rows, width), F32),
            ]
            + [vmem((width, units), BF16)] * 3
            + reduce_scratch(size, units) * 3
            + [arrived, arrived, dma, dma, dma((2, 3, 10)), dma((2, 4, n_tensor - 1))],
            5,
            vmem=60,
        )

    tile = struct((rows, local))
    grad_query_b, grad_key_b, grad_value_b, grad_text_all, gain_sums = run(
        functools.partial(attend_back_kernel, micro, scale),
        [tile, tile, tile, struct((2 * local, images * TXT)), struct((8, local), F32)],
        scalars(live, lens)
        + outside(
            grad_mixed, cross_out, query_rot, key_rot, value, text_key, text_value, text_raw,
            query_raw, key_raw,
        )
        + inside(query_gain, key_gain, text_gain)
        + outside(cosine, sine)
        + inside(self_id, self_row, segment, gate),
        [
            vmem((rows, local), F32),
            vmem((rows, local), F32),
            vmem((rows, local), BF16),
            vmem((local, TXT), F32),
            vmem((local, TXT), F32),
            vmem((images, TXT, local), BF16),
            vmem((images, TXT, local), BF16),
            vmem((images, TXT, local), BF16),
            dma((3,)),
        ]
        + [vmem((rows, local), F32)] * 2
        + [vmem((rows, local), BF16)] * 3
        + [vmem((rows, local), F32)] * 4
        + [
            dma((9,)),
        ],
        flops=4 * 2**30,
        traffic=15 * 2**20,
    )

    total_qv, total_ko, attn_in_part = run(
        attn_grad_kernel,
        [struct((width, 2 * local))] * 2 + [struct((rows, width))],
        inside(attn_in, grad_query_b, grad_key_b, grad_value_b, grad_attn_out, mixed)
        + outside(whole_qv, whole_ko),
        [
            vmem((width, 2 * local), BF16),
            vmem((width, 2 * local), BF16),
            vmem((rows, 2 * local), BF16),
            dma((2,)),
        ],
        flops=14 * rows * width * local,
        traffic=15 * 2**20,
    )
    depth = DT // parts
    caption_rows = captions.reshape(images * TXT, DT)
    if parts == 1:
        grad_attn_in = lax.psum(attn_in_part, "tensor")
        grad_text = dot_nn(grad_text_all, caption_rows)
        wholes = (total_qv, total_ko, grad_text.T)
        grad_qv, grad_ko, grad_text = [scattered(whole.astype(F32)) for whole in wholes]
        grad_query, grad_value = grad_qv[:, :local], grad_qv[:, local:]
        grad_key, grad_out = grad_ko[:, :local], grad_ko[:, local:]
        grad_tk, grad_tv = grad_text[:, :local], grad_text[:, local:]
        grad_f = [grad_f[:, i * units : (i + 1) * units] for i in range(3)]
        result, ffn_mod, ffn_gain_sum = run(
            output_kernel,
            [struct((rows, width)), struct((padded, width), F32), struct((1, width), F32)],
            inside(hidden, member, ffn_gain, grad_y, mods, ffn_out, grad_ffn_in),
            [wide, wide, vmem((rows, width), F32)],
        )
        grad_tokens, grad_mod, attn_gain_sum = run(
            input_kernel,
            [struct((rows, width)), struct((padded, width)), struct((1, width), F32)],
            inside(
                token_rows, member, attn_gain, grad_hidden, ffn_mod, mods, grad_attn_in, attn_out
            ),
            [wide, wide, vmem((rows, width), F32)],
        )
        grad_w_adaln = dot_tn(cond_act, gathered(grad_mod[:images]))
        sums = [attn_gain_sum[0], ffn_gain_sum[0]]
        sums += [row.reshape(heads, HEAD_DIM).T for row in gain_sums[:3]]
        sums = lax.psum(sums, "dp")
        own = [
            lax.dynamic_slice_in_dim(whole, dp_rank * (whole.shape[0] // n_dp), whole.shape[0] // n_dp, 0)
            for whole in sums
        ]
        own.append(lax.psum(jnp.sum(gain_sums[3].reshape(heads, HEAD_DIM), axis=1), "dp"))
    else:
        grad_qv, grad_ko, grad_text, result, grad_tokens, grad_w_adaln, *own = exchange(
            functools.partial(last_exchange_kernel, n_tensor),
            [
                (struct((size, 2 * local), F32), vmem),
                (struct((size, 2 * local), F32), vmem),
                (struct((2 * local, depth), F32), vmem),
                (struct((rows, width)), vmem),
                (struct((rows, width)), vmem),
                (struct((cond_rows, span), F32), vmem),
            ]
            + [(struct((1, gain_attn.size), F32), vmem)] * 2
            + [(struct(gain_query.shape, F32), vmem)] * 3
            + [(struct((1, heads), F32), vmem)],
            outside(
                caption_rows, grad_text_all, total_qv, total_ko, token_rows, grad_hidden, attn_out
            )
            + inside(
                attn_in_part, member, attn_gain, mods, cond_act, gain_sums, result_rows, gate_part, ffn_mod,
                ffn_gain_sum,
            ),
            reduce_scratch(size, 2 * local) * 2
            + reduce_scratch(2 * local, depth)
            + [
                vmem((parts, 2 * local, depth), BF16),
                vmem((2, images * TXT, depth), BF16),
                wide,
                vmem((n_tensor, padded, width), BF16),
                vmem((padded, width), F32),
                vmem((padded, width), BF16),
                arrived,
                wide,
                wide,
                vmem((rows, width), F32),
                vmem((2, width), F32),
                vmem((1, width), F32),
                vmem((parts, padded, width), BF16),
                vmem((parts, 2, width), F32),
                vmem((parts, 1, width), F32),
                vmem((8, 128), F32),
                dma((2,)),
                dma((2, 3, 10)),
                dma((2, 4, n_tensor - 1)),
                dma((2, 3, 8)),
                vmem((2 * local, images * TXT), BF16),
                vmem((width, 2 * local), BF16),
                vmem((width, 2 * local), BF16),
                wide,
                vmem((rows, width), F32),
                wide,
                dma((6,)),
            ],
            3,
            vmem=62,
        )
        own[:2] = [part[0] for part in own[:2]]
        own[5] = own[5][0]
        plain = [*grad_f, grad_w_adaln, result, grad_tokens]
        square, tall = struct((size, local), F32), struct((depth, local), F32)
        (
            grad_query, grad_key, grad_value, grad_out, grad_tk, grad_tv, *plain
        ) = pl.pallas_call(
            emit_kernel,
            out_shape=[square] * 4 + [tall] * 2 + [struct(x.shape, x.dtype) for x in plain],
            in_specs=[pl.BlockSpec(memory_space=anywhere)] * (3 + len(plain)),
            out_specs=[pl.BlockSpec(memory_space=anywhere)] * (6 + len(plain)),
            scratch_shapes=[vmem(x.shape, x.dtype) for x in (grad_qv, grad_ko, grad_text, *plain)]
            + [
                vmem((depth, local), F32),
                vmem((depth, local), F32),
                dma((3 + len(plain),)),
                dma((6 + len(plain),)),
            ],
            compiler_params=pltpu.CompilerParams(vmem_limit_bytes=62 * 2**20),
        )(grad_qv, grad_ko, grad_text, *plain)
        *grad_f, grad_w_adaln, result, grad_tokens = plain

    return (
        result.reshape(micro, count, width),
        grad_tokens.reshape(micro, count, width),
        grad_query,
        grad_key,
        grad_value,
        grad_out,
        grad_tk,
        grad_tv,
        *grad_f,
        grad_w_adaln,
        *own,
    )


def solution(mesh):
    return jax.shard_map(
        functools.partial(shards, mesh.shape["dp"], mesh.shape["tensor"]),
        mesh=mesh,
        in_specs=(
            P(None, "dp", None),
            P(None, "dp", None),
            P(None, "dp", None, None),
            P(None, "dp", None),
            P(None, "dp"),
            P("dp", "tensor"),
            P("dp", "tensor"),
            P("dp", "tensor"),
            P("dp", "tensor"),
            P("dp", "tensor"),
            P("dp", "tensor"),
            P("dp", "tensor"),
            P("dp", "tensor"),
            P("dp", "tensor"),
            P("dp", "tensor"),
            P("dp"),
            P("dp"),
            P("dp", "tensor"),
            P("dp", "tensor"),
            P("dp", "tensor"),
            P("tensor"),
            P(None, "dp", None),
        ),
        out_specs=(
            P(None, "dp", None),
            P(None, "dp", None),
            P("dp", "tensor"),
            P("dp", "tensor"),
            P("dp", "tensor"),
            P("dp", "tensor"),
            P("dp", "tensor"),
            P("dp", "tensor"),
            P("dp", "tensor"),
            P("dp", "tensor"),
            P("dp", "tensor"),
            P("dp", "tensor"),
            P("dp"),
            P("dp"),
            P("dp", "tensor"),
            P("dp", "tensor"),
            P("dp", "tensor"),
            P("tensor"),
        ),
        check_vma=False,
    )
```

profile of v0, /device:TPU:8, one launch (start us, length us, event | category | flops | bytes accessed | tf_op | source)
XLA Modules:
  0.0 339.7 jit_solution(14910949373560308628)
XLA Ops:
  7.3 0.9 broadcast_in_dim.30.attn_own
  8.2 0.7 broadcast_in_dim.31.ffn_own
  8.9 0.7 copy.53.context
  9.6 2.4 pad_maximum_fusion
  12.2 71.0 %shard_map.349 = (bf16[12,256,384]{2,1,0:T(8,128)(2,1)S(1)}, bf16[12,256,384]{2,1,0:T(8,128)(2,1)}, bf16[12,256,384]{2,1,0:T(8,128)(2,1)}, bf16[1536,768]{1,0:T(...) custom-call(bf16[512,384]{1,0:T(8,128)(2,1)S(1)} %copy-done.6, ...), custom_call_target="tpu_custom_call" | custom-call | tf_op jit(solution)/shard_map/pallas_call | solution.py:611
  83.2 0.6 copy-done.9
  83.8 1.4 copy-done.16
  88.2 15.4 %shard_map.350 = (bf16[256,1536]{1,0:T(8,128)(2,1)S(1)}, f32[256,384]{1,0:T(8,128)S(1)}, f32[256,384]{1,0:T(8,128)S(1)}, bf16[256,384]{1,0:T(8,128)(2,1)S(1)}, b...) custom-call(bf16[256,1536]{1,0:T(8,128)(2,1)S(1)} %bitcast.100, bf16[256,16]{1,0:T(8,128)(2,1)S(1)} %pad.5.member, ...), custom_call_target="tpu_custom_call" | custom-call | flops 905969664 | bytes 10485760 | tf_op jit(solution)/shard_map/pallas_call | solution.py:70
  103.6 0.7 copy-done.20
  104.4 10.8 %shard_map.351 = (bf16[256,384]{1,0:T(8,128)(2,1)S(1)}, f32[256,384]{1,0:T(8,128)S(1)}, bf16[256,1536]{1,0:T(8,128)(2,1)S(1)}) custom-call(s32[12]{0:T(128)S(1)} %or_convert_fusion.live, s32[12]{0:T(128)S(1)} %reshape.690.text_len, bf16[256,384]{1,0:T(8,128)(2,1)S(1)} %get-tuple-element.89.query, bf16[256,384]{1,0:T(8,128)(2,1)S(1)} %get-tuple-element.90.key, ...), custom_call_target="tpu_custom_call" | custom-call | flops 2147483648 | bytes 12582912 | tf_op jit(solution)/shard_map/pallas_call | solution.py:70
  115.2 0.7 copy-done.31
  116.0 0.7 copy-done.33
  116.7 39.1 %shard_map.352.attn_out.attn_far = bf16[256,1536]{1,0:T(8,128)(2,1)S(1)} custom-call(bf16[256,1536]{1,0:T(8,128)(2,1)S(1)} %get-tuple-element.94.partial), custom_call_target="tpu_custom_call" | custom-call | tf_op jit(solution)/shard_map/pallas_call | solution.py:611
  155.7 0.9 copy-done
  156.6 65.4 %shard_map.353 = (f32[256,1536]{1,0:T(8,128)}, f32[256,1536]{1,0:T(8,128)}, bf16[256,1536]{1,0:T(8,128)(2,1)}, f32[256,384]{1,0:T(8,128)}, bf16[64,1536]{1,0:T(8...) custom-call(bf16[256,1536]{1,0:T(8,128)(2,1)} %bitcast.98, ...), custom_call_target="tpu_custom_call" | custom-call | tf_op jit(solution)/shard_map/pallas_call | solution.py:611
  222.1 1.7 copy-done.18
  223.7 1.0 copy-done.24
  224.7 0.9 copy-done.26
  225.7 0.9 copy-done.28
  226.6 0.9 copy-done.30
  227.5 1.0 copy-done.32
  228.5 19.4 %shard_map.354 = (bf16[256,384]{1,0:T(8,128)(2,1)S(1)}, bf16[256,384]{1,0:T(8,128)(2,1)S(1)}, bf16[256,384]{1,0:T(8,128)(2,1)S(1)}, bf16[768,3072]{1,0:T(8,128)(2,1)}, f32[8,384]{1,0:T(8,128)S(1)}) custom-call(s32[12]{0:T(128)S(1)} %or_convert_fusion.live, s32[12]{0:T(128)S(1)} %reshape.690.text_len, f32[256,384]{1,0:T(8,128)S(1)} %copy-done.24, ...), custom_call_target="tpu_custom_call" | custom-call | flops 4294967296 | bytes 15728640 | tf_op jit(solution)/shard_map/pallas_call | solution.py:70
  248.0 0.6 copy-done.11
  248.6 6.5 %shard_map.355 = (bf16[1536,768]{1,0:T(8,128)(2,1)S(1)}, bf16[1536,768]{1,0:T(8,128)(2,1)}, bf16[256,1536]{1,0:T(8,128)(2,1)S(1)}) custom-call(bf16[256,1536]{1,0:T(8,128)(2,1)S(1)} %get-tuple-element.103.attn_in, bf16[256,384]{1,0:T(8,128)(2,1)S(1)} %get-tuple-element.104.grad_query, bf16[256,384]{1,0:T(8,128)(2,1)S(1)} %get-tuple-element.105.grad_key, ...), custom_call_target="tpu_custom_call" | custom-call | flops 2113929216 | bytes 15728640 | tf_op jit(solution)/shard_map/pallas_call | solution.py:70
  255.1 1.5 copy-done.2
  256.5 0.9 copy-done.5
  257.4 66.1 %shard_map.356 = (f32[192,768]{1,0:T(8,128)}, f32[192,768]{1,0:T(8,128)}, f32[768,512]{1,0:T(8,128)}, bf16[256,1536]{1,0:T(8,128)(2,1)}, bf16[256,1536]{1,0:T(8,...) custom-call(bf16[3072,4096]{1,0:T(8,128)(2,1)} %bitcast.102, ...), custom_call_target="tpu_custom_call" | custom-call | tf_op jit(solution)/shard_map/pallas_call | solution.py:611
  323.6 5.6 %shard_map.357 = (f32[192,384]{1,0:T(8,128)}, f32[192,384]{1,0:T(8,128)}, f32[192,384]{1,0:T(8,128)}, f32[192,384]{1,0:T(8,128)}, f32[512,384]{1,0:T(8,128)}, /*...) custom-call(f32[192,768]{1,0:T(8,128)} %get-tuple-element.119.refs_0, ...), custom_call_target="tpu_custom_call" | custom-call | tf_op jit(solution)/shard_map/pallas_call | solution.py:1698
  329.2 0.6 copy.73
  330.4 0.6 copy.75
  330.9 0.6 copy.76
  331.5 0.6 copy.77
  (133 shorter events, 4.1 us)
Async XLA Ops:
  7.2 4.8 %copy-start.37 = (bf16[192,384]{1,0:T(8,128)(2,1)S(1)}, bf16[192,384]{1,0:T(8,128)(2,1)}, u32[]{:S(2)}) copy-start(bf16[192,384]{1,0:T(8,128)(2,1)} %param.30) | copy-start | bytes 442372
  7.2 4.8 %copy-start.35 = (bf16[192,384]{1,0:T(8,128)(2,1)S(1)}, bf16[192,384]{1,0:T(8,128)(2,1)}, u32[]{:S(2)}) copy-start(bf16[192,384]{1,0:T(8,128)(2,1)} %param.29) | copy-start | bytes 442372
  7.2 4.8 %copy-start.38 = (bf16[192,384]{1,0:T(8,128)(2,1)S(1)}, bf16[192,384]{1,0:T(8,128)(2,1)}, u32[]{:S(2)}) copy-start(bf16[192,384]{1,0:T(8,128)(2,1)} %param.28) | copy-start | bytes 442372
  7.2 4.8 %copy-start.36 = (bf16[192,384]{1,0:T(8,128)(2,1)S(1)}, bf16[192,384]{1,0:T(8,128)(2,1)}, u32[]{:S(2)}) copy-start(bf16[192,384]{1,0:T(8,128)(2,1)} %param.27) | copy-start | bytes 442372
  7.2 4.8 %copy-start.15 = (bf16[8,6]{1,0:T(8,128)(2,1)S(1)}, bf16[8,6]{1,0:T(8,128)(2,1)}, u32[]{:S(2)}) copy-start(bf16[8,6]{1,0:T(8,128)(2,1)} %t_own.1) | copy-start | bytes 292
  7.2 4.8 %copy-start.14 = (bf16[8,6]{1,0:T(8,128)(2,1)S(1)}, bf16[8,6]{1,0:T(8,128)(2,1)}, u32[]{:S(2)}) copy-start(bf16[8,6]{1,0:T(8,128)(2,1)} %k_own.1) | copy-start | bytes 292
  7.3 4.8 %copy-start.13 = (bf16[8,6]{1,0:T(8,128)(2,1)S(1)}, bf16[8,6]{1,0:T(8,128)(2,1)}, u32[]{:S(2)}) copy-start(bf16[8,6]{1,0:T(8,128)(2,1)} %q_own.1) | copy-start | bytes 292
  7.3 4.8 %copy-start.8 = (bf16[128,1536]{1,0:T(8,128)(2,1)S(1)}, bf16[128,1536]{1,0:T(8,128)(2,1)}, u32[]{:S(2)}) copy-start(bf16[128,1536]{1,0:T(8,128)(2,1)} %w_adaln.1) | copy-start | bytes 1179652
  7.3 4.8 %copy-start.7 = (bf16[512,384]{1,0:T(8,128)(2,1)S(1)}, bf16[512,384]{1,0:T(8,128)(2,1)}, u32[]{:S(2)}) copy-start(bf16[512,384]{1,0:T(8,128)(2,1)} %shard_tv.1) | copy-start | bytes 1179652
  7.3 4.8 %copy-start.6 = (bf16[512,384]{1,0:T(8,128)(2,1)S(1)}, bf16[512,384]{1,0:T(8,128)(2,1)}, u32[]{:S(2)}) copy-start(bf16[512,384]{1,0:T(8,128)(2,1)} %shard_tk.1) | copy-start | bytes 1179652
  7.3 149.3 %all-gather.2.cloned.1.call-start = ((), (), s32[]{:S(2)}) async-start(), calls=%async_computation | async-start | bytes 10616832 | tf_op jit(solution)/shard_map/all_gather | solution.py:1320
  12.1 73.1 %copy-start.45 = (s32[2,6]{1,0:T(2,128)S(1)}, s32[2,6]{1,0:T(2,128)}, u32[]{:S(2)}) copy-start(s32[2,6]{1,0:T(2,128)} %param.26) | copy-start | bytes 148
  12.1 73.2 %copy-start.39 = (s32[2,6,2]{1,2,0:T(2,128)S(1)}, s32[2,6,2]{1,2,0:T(2,128)}, u32[]{:S(2)}) copy-start(s32[2,6,2]{1,2,0:T(2,128)} %param.25) | copy-start | bytes 292
  12.1 74.3 %copy-start.46 = (bf16[6]{0:T(256)(128)(2,1)S(1)}, bf16[6]{0:T(256)(128)(2,1)}, u32[]{:S(2)}) copy-start(bf16[6]{0:T(256)(128)(2,1)} %param.42) | copy-start | bytes 40
  85.2 18.3 %copy-start.3 = (bf16[4,16,1536]{2,1,0:T(8,128)(2,1)}, bf16[4,16,1536]{2,1,0:T(8,128)(2,1)S(1)}, u32[]{:S(2)}) copy-start(bf16[4,16,1536]{2,1,0:T(8,128)(2,1)S(1)} %get-tuple-element.83.mods) | copy-start | bytes 589828
  85.2 18.4 %copy-start.10 = (f32[1,1536]{1,0:T(1,128)}, f32[1,1536]{1,0:T(1,128)S(1)}, u32[]{:S(2)}) copy-start(f32[1,1536]{1,0:T(1,128)S(1)} %get-tuple-element.84.gain.attn_gain) | copy-start | bytes 18436
  87.0 16.6 %copy-start.4 = (bf16[256,16]{1,0:T(8,128)(2,1)}, bf16[256,16]{1,0:T(8,128)(2,1)S(1)}, u32[]{:S(2)}) copy-start(bf16[256,16]{1,0:T(8,128)(2,1)S(1)} %pad.5.member) | copy-start | bytes 24580
  88.1 16.2 %copy-start.17 = (bf16[12,256,384]{2,1,0:T(8,128)(2,1)S(1)}, bf16[12,256,384]{2,1,0:T(8,128)(2,1)}, u32[]{:S(2)}) copy-start(bf16[12,256,384]{2,1,0:T(8,128)(2,1)} %get-tuple-element.92.text_key_far) | copy-start | bytes 7077892
  104.3 10.8 %copy-start.22 = (f32[256,384]{1,0:T(8,128)}, f32[256,384]{1,0:T(8,128)S(1)}, u32[]{:S(2)}) copy-start(f32[256,384]{1,0:T(8,128)S(1)} %get-tuple-element.100.key_raw) | copy-start | bytes 1179652
  104.3 10.9 %copy-start.25 = (bf16[256,384]{1,0:T(8,128)(2,1)}, bf16[256,384]{1,0:T(8,128)(2,1)S(1)}, u32[]{:S(2)}) copy-start(bf16[256,384]{1,0:T(8,128)(2,1)S(1)} %get-tuple-element.89.query) | copy-start | bytes 589828
  104.3 10.9 %copy-start.27 = (bf16[256,384]{1,0:T(8,128)(2,1)}, bf16[256,384]{1,0:T(8,128)(2,1)S(1)}, u32[]{:S(2)}) copy-start(bf16[256,384]{1,0:T(8,128)(2,1)S(1)} %get-tuple-element.90.key) | copy-start | bytes 589828
  104.4 10.9 %copy-start.29 = (bf16[256,384]{1,0:T(8,128)(2,1)}, bf16[256,384]{1,0:T(8,128)(2,1)S(1)}, u32[]{:S(2)}) copy-start(bf16[256,384]{1,0:T(8,128)(2,1)S(1)} %get-tuple-element.91.value) | copy-start | bytes 589828
  156.6 65.5 %copy-start.21 = (f32[256,384]{1,0:T(8,128)S(1)}, f32[256,384]{1,0:T(8,128)}, u32[]{:S(2)}) copy-start(f32[256,384]{1,0:T(8,128)} %copy-done.20) | copy-start | bytes 1179652
  156.6 65.5 %copy-start.23 = (f32[256,384]{1,0:T(8,128)S(1)}, f32[256,384]{1,0:T(8,128)}, u32[]{:S(2)}) copy-start(f32[256,384]{1,0:T(8,128)} %copy-done.22) | copy-start | bytes 1179652
  228.5 20.0 %copy-start.19 = (bf16[256,1536]{1,0:T(8,128)(2,1)S(1)}, bf16[256,1536]{1,0:T(8,128)(2,1)}, u32[]{:S(2)}) copy-start(bf16[256,1536]{1,0:T(8,128)(2,1)} %get-tuple-element.107.grad_out) | copy-start | bytes 2359300
  228.5 20.0 %copy-start.34 = (bf16[256,384]{1,0:T(8,128)(2,1)S(1)}, bf16[256,384]{1,0:T(8,128)(2,1)}, u32[]{:S(2)}) copy-start(bf16[256,384]{1,0:T(8,128)(2,1)} %copy-done.33) | copy-start | bytes 589828
  323.5 5.7 %copy-start.44 = (f32[1,192]{1,0:T(1,128)S(1)}, f32[1,192]{1,0:T(1,128)}, u32[]{:S(2)}) copy-start(f32[1,192]{1,0:T(1,128)} %get-tuple-element.140) | copy-start | bytes 2308
  323.5 6.3 %copy-start.43 = (f32[1,192]{1,0:T(1,128)S(1)}, f32[1,192]{1,0:T(1,128)}, u32[]{:S(2)}) copy-start(f32[1,192]{1,0:T(1,128)} %get-tuple-element.141) | copy-start | bytes 2308
  323.5 6.8 %copy-start.42 = (f32[8,6]{1,0:T(8,128)S(1)}, f32[8,6]{1,0:T(8,128)}, u32[]{:S(2)}) copy-start(f32[8,6]{1,0:T(8,128)} %get-tuple-element.207) | copy-start | bytes 580
  323.5 7.4 %copy-start.41 = (f32[8,6]{1,0:T(8,128)S(1)}, f32[8,6]{1,0:T(8,128)}, u32[]{:S(2)}) copy-start(f32[8,6]{1,0:T(8,128)} %get-tuple-element.208) | copy-start | bytes 580
  323.5 8.0 %copy-start.40 = (f32[8,6]{1,0:T(8,128)S(1)}, f32[8,6]{1,0:T(8,128)}, u32[]{:S(2)}) copy-start(f32[8,6]{1,0:T(8,128)} %get-tuple-element.209) | copy-start | bytes 580
  323.5 8.6 %copy-start.47 = (f32[1,6]{1,0:T(1,128)S(1)}, f32[1,6]{1,0:T(1,128)}, u32[]{:S(2)}) copy-start(f32[1,6]{1,0:T(1,128)} %get-tuple-element.145) | copy-start | bytes 76
  (17 other events, 19.0 us)
Sparse Core Ops, SparseCore 0:
  85.4 58.4 all-gather.1
where the time goes:
time: 345 us; the launch traced here: 340 us
  Pallas kernels  299 us (87%)
  local copies, waits for them, and re-layouts  21.6 us (6%)
  between operations  14.9 us (4%)
  other arithmetic  3.82 us (1%)
    pallas_call x4, Pallas kernels, exchange(): pl.pallas_call(body, out_shape=[shape for shape, _ in outs], in_specs=[pl...  242 us
    pallas_call x4, Pallas kernels, run(): pl.pallas_call(body, out_shape=outs, in_specs=[pl.BlockSpec(memory_space=...  52.1 us
    unnamed x107, local copies, waits for them, and re-layouts  18.9 us
  transfers between devices with their start and end apart: 1, of which 0 were waited for; matrix products, arithmetic and copies ran while one was open for 1% of the time, Pallas kernels for 19%

commit v1 on v0

--- a/solution.py
+++ b/solution.py
@@ -66,14 +66,14 @@
     return jax.ShapeDtypeStruct(shape, dtype)
 
 
-def run(body, outs, ins, scratch=(), flops=0, traffic=0):
+def run(body, outs, ins, scratch=(), flops=0, traffic=0, vmem=48):
     return pl.pallas_call(
         body,
         out_shape=outs,
         in_specs=[pl.BlockSpec(memory_space=space) for _, space in ins],
         out_specs=[pl.BlockSpec(memory_space=pltpu.VMEM)] * len(outs),
         scratch_shapes=list(scratch),
-        compiler_params=pltpu.CompilerParams(vmem_limit_bytes=48 * 2**20),
+        compiler_params=pltpu.CompilerParams(vmem_limit_bytes=vmem * 2**20),
         cost_estimate=pl.CostEstimate(flops=flops, bytes_accessed=traffic, transcendentals=0),
     )(*[array for array, _ in ins])
 
@@ -1584,6 +1584,7 @@
         ],
         flops=4 * 2**30,
         traffic=15 * 2**20,
+        vmem=62,
     )
 
     total_qv, total_ko, attn_in_part = run(

time: 345 us -> 343 us (level)
  local copies, waits for them, and re-layouts: 21.6 us -> 17.8 us
    pallas_call x4, Pallas kernels: 242 us -> 246 us  [exchange(): pl.pallas_call(body, out_shape=[shape for shape, _ in outs], in_specs=[pl...]
    pallas_call x4, Pallas kernels: 52.1 us -> 47.8 us  [run(): pl.pallas_call(body, out_shape=outs, in_specs=[pl.BlockSpec(memory_space=...]
    unnamed x107 -> x117, local copies, waits for them, and re-layouts: 18.9 us -> 15.2 us
where the time goes in v1:
time: 343 us; the launch traced here: 337 us
  Pallas kernels  300 us (87%)
  local copies, waits for them, and re-layouts  17.8 us (5%)
  between operations  15.1 us (4%)
  other arithmetic  3.81 us (1%)
    pallas_call x4, Pallas kernels, exchange(): pl.pallas_call(body, out_shape=[shape for shape, _ in outs], in_specs=[pl...  246 us
    pallas_call x4, Pallas kernels, run(): pl.pallas_call(body, out_shape=outs, in_specs=[pl.BlockSpec(memory_space=...  47.8 us
    unnamed x117, local copies, waits for them, and re-layouts  15.2 us
  transfers between devices with their start and end apart: 1, of which 0 were waited for; matrix products, arithmetic and copies ran while one was open for 1% of the time, Pallas kernels for 19%

profile of v1, /device:TPU:8, one launch (start us, length us, event | category | flops | bytes accessed | tf_op | source)
XLA Modules:
  0.0 336.6 jit_solution(6603589247916483429)
XLA Ops:
  7.3 0.9 broadcast_in_dim.30.attn_own
  8.2 0.7 broadcast_in_dim.31.ffn_own
  8.9 0.7 copy.53.context
  9.6 2.4 pad_maximum_fusion
  12.2 71.0 %shard_map.349 = (bf16[12,256,384]{2,1,0:T(8,128)(2,1)S(1)}, bf16[12,256,384]{2,1,0:T(8,128)(2,1)}, bf16[12,256,384]{2,1,0:T(8,128)(2,1)}, bf16[1536,768]{1,0:T(...) custom-call(bf16[512,384]{1,0:T(8,128)(2,1)S(1)} %copy-done.9, ...), custom_call_target="tpu_custom_call" | custom-call | tf_op jit(solution)/shard_map/pallas_call | solution.py:611
  83.2 0.6 copy-done.13
  83.8 0.6 copy-done.15
  84.4 1.4 copy-done.23
  85.8 0.6 copy-done.33
  86.8 0.2 reduce-window.14
  89.4 16.5 %shard_map.350 = (bf16[256,1536]{1,0:T(8,128)(2,1)S(1)}, f32[256,384]{1,0:T(8,128)S(1)}, f32[256,384]{1,0:T(8,128)S(1)}, bf16[256,384]{1,0:T(8,128)(2,1)S(1)}, b...) custom-call(bf16[256,1536]{1,0:T(8,128)(2,1)S(1)} %bitcast.100, bf16[256,16]{1,0:T(8,128)(2,1)S(1)} %pad.5.member, ...), custom_call_target="tpu_custom_call" | custom-call | flops 905969664 | bytes 10485760 | tf_op jit(solution)/shard_map/pallas_call | solution.py:70
  106.0 0.7 copy-done.28
  106.9 8.1 %shard_map.351 = (bf16[256,384]{1,0:T(8,128)(2,1)S(1)}, f32[256,384]{1,0:T(8,128)S(1)}, bf16[256,1536]{1,0:T(8,128)(2,1)S(1)}) custom-call(s32[12]{0:T(128)S(1)} %or_convert_fusion.live, s32[12]{0:T(128)S(1)} %reshape.690.text_len, bf16[256,384]{1,0:T(8,128)(2,1)S(1)} %get-tuple-element.89.query, bf16[256,384]{1,0:T(8,128)(2,1)S(1)} %get-tuple-element.90.key, ...), custom_call_target="tpu_custom_call" | custom-call | flops 2147483648 | bytes 12582912 | tf_op jit(solution)/shard_map/pallas_call | solution.py:70
  115.1 0.7 copy-done.36
  115.8 37.9 %shard_map.352.attn_out.attn_far = bf16[256,1536]{1,0:T(8,128)(2,1)S(1)} custom-call(bf16[256,1536]{1,0:T(8,128)(2,1)S(1)} %get-tuple-element.94.partial), custom_call_target="tpu_custom_call" | custom-call | tf_op jit(solution)/shard_map/pallas_call | solution.py:611
  153.8 0.9 copy-done
  154.7 65.6 %shard_map.353 = (f32[256,1536]{1,0:T(8,128)}, f32[256,1536]{1,0:T(8,128)}, bf16[256,1536]{1,0:T(8,128)(2,1)}, f32[256,384]{1,0:T(8,128)}, bf16[64,1536]{1,0:T(8...) custom-call(bf16[256,1536]{1,0:T(8,128)(2,1)} %bitcast.98, ...), custom_call_target="tpu_custom_call" | custom-call | tf_op jit(solution)/shard_map/pallas_call | solution.py:611
  220.3 16.7 %shard_map.354 = (bf16[256,384]{1,0:T(8,128)(2,1)}, bf16[256,384]{1,0:T(8,128)(2,1)}, bf16[256,384]{1,0:T(8,128)(2,1)}, bf16[768,3072]{1,0:T(8,128)(2,1)}, f32[8,384]{1,0:T(8,128)}) custom-call(s32[12]{0:T(128)} %copy-done.35, s32[12]{0:T(128)} %copy-done.34, f32[256,384]{1,0:T(8,128)} %get-tuple-element.96.grad_mixed, f32[256,384]{1,0:T(8,128)} %copy-done.36, ...), custom_call_target="tpu_custom_call" | custom-call | flops 4294967296 | bytes 15728640 | tf_op jit(solution)/shard_map/pallas_call | solution.py:70
  237.0 0.9 copy-done.37
  238.0 0.9 copy-done.38
  238.9 0.9 copy-done.39
  239.8 6.5 %shard_map.355 = (bf16[1536,768]{1,0:T(8,128)(2,1)S(1)}, bf16[1536,768]{1,0:T(8,128)(2,1)}, bf16[256,1536]{1,0:T(8,128)(2,1)S(1)}) custom-call(bf16[256,1536]{1,0:T(8,128)(2,1)S(1)} %copy-done.26, bf16[256,384]{1,0:T(8,128)(2,1)S(1)} %copy-done.37, bf16[256,384]{1,0:T(8,128)(2,1)S(1)} %copy-done.38, bf16[256,384]{1,0:T(8,128)(2,1)S(1)} %copy-done.39, ...), custom_call_target="tpu_custom_call" | custom-call | flops 2113929216 | bytes 15728640 | tf_op jit(solution)/shard_map/pallas_call | solution.py:70
  246.3 1.4 copy-done.2
  247.7 0.9 copy-done.7
  248.6 71.8 %shard_map.356 = (f32[192,768]{1,0:T(8,128)}, f32[192,768]{1,0:T(8,128)}, f32[768,512]{1,0:T(8,128)}, bf16[256,1536]{1,0:T(8,128)(2,1)}, bf16[256,1536]{1,0:T(8,...) custom-call(bf16[3072,4096]{1,0:T(8,128)(2,1)} %bitcast.102, ...), custom_call_target="tpu_custom_call" | custom-call | tf_op jit(solution)/shard_map/pallas_call | solution.py:611
  320.5 5.6 %shard_map.357 = (f32[192,384]{1,0:T(8,128)}, f32[192,384]{1,0:T(8,128)}, f32[192,384]{1,0:T(8,128)}, f32[192,384]{1,0:T(8,128)}, f32[512,384]{1,0:T(8,128)}, /*...) custom-call(f32[192,768]{1,0:T(8,128)} %get-tuple-element.119.refs_0, ...), custom_call_target="tpu_custom_call" | custom-call | tf_op jit(solution)/shard_map/pallas_call | solution.py:1699
  326.1 0.6 copy.73
  326.7 0.6 copy.74
  327.3 0.6 copy.75
  327.9 0.6 copy.76
  328.4 0.6 copy.77
  329.0 0.5 copy.78
  (143 shorter events, 2.8 us)
Async XLA Ops:
  7.2 4.8 %copy-start.18 = (bf16[8,6]{1,0:T(8,128)(2,1)S(1)}, bf16[8,6]{1,0:T(8,128)(2,1)}, u32[]{:S(2)}) copy-start(bf16[8,6]{1,0:T(8,128)(2,1)} %t_own.1) | copy-start | bytes 292
  7.3 147.4 %all-gather.2.cloned.1.call-start = ((), (), s32[]{:S(2)}) async-start(), calls=%async_computation | async-start | bytes 10616832 | tf_op jit(solution)/shard_map/all_gather | solution.py:1320
  12.1 74.3 %copy-start.50 = (s32[2,6]{1,0:T(2,128)S(1)}, s32[2,6]{1,0:T(2,128)}, u32[]{:S(2)}) copy-start(s32[2,6]{1,0:T(2,128)} %param.26) | copy-start | bytes 148
  12.1 74.4 %copy-start.44 = (s32[2,6,2]{1,2,0:T(2,128)S(1)}, s32[2,6,2]{1,2,0:T(2,128)}, u32[]{:S(2)}) copy-start(s32[2,6,2]{1,2,0:T(2,128)} %param.25) | copy-start | bytes 292
  12.1 75.5 %copy-start.51 = (bf16[6]{0:T(256)(128)(2,1)S(1)}, bf16[6]{0:T(256)(128)(2,1)}, u32[]{:S(2)}) copy-start(bf16[6]{0:T(256)(128)(2,1)} %param.42) | copy-start | bytes 40
  86.4 19.5 %copy-start.3 = (bf16[4,16,1536]{2,1,0:T(8,128)(2,1)}, bf16[4,16,1536]{2,1,0:T(8,128)(2,1)S(1)}, u32[]{:S(2)}) copy-start(bf16[4,16,1536]{2,1,0:T(8,128)(2,1)S(1)} %get-tuple-element.83.mods) | copy-start | bytes 589828
  86.4 19.5 %copy-start.14 = (f32[1,1536]{1,0:T(1,128)}, f32[1,1536]{1,0:T(1,128)S(1)}, u32[]{:S(2)}) copy-start(f32[1,1536]{1,0:T(1,128)S(1)} %get-tuple-element.84.gain.attn_gain) | copy-start | bytes 18436
  86.4 19.5 %copy-start.19 = (f32[1,384]{1,0:T(1,128)}, f32[1,384]{1,0:T(1,128)S(1)}, u32[]{:S(2)}) copy-start(f32[1,384]{1,0:T(1,128)S(1)} %get-tuple-element.85.q_gain) | copy-start | bytes 4612
  86.4 19.6 %copy-start.20 = (f32[1,384]{1,0:T(1,128)}, f32[1,384]{1,0:T(1,128)S(1)}, u32[]{:S(2)}) copy-start(f32[1,384]{1,0:T(1,128)S(1)} %get-tuple-element.86.k_gain) | copy-start | bytes 4612
  86.5 20.3 %copy-start.34 = (s32[12]{0:T(128)}, s32[12]{0:T(128)S(1)}, u32[]{:S(2)}) copy-start(s32[12]{0:T(128)S(1)} %reshape.690.text_len) | copy-start | bytes 148
  87.8 19.0 %copy-start.21 = (f32[1,384]{1,0:T(1,128)}, f32[1,384]{1,0:T(1,128)S(1)}, u32[]{:S(2)}) copy-start(f32[1,384]{1,0:T(1,128)S(1)} %broadcast_in_dim_reshape.3.gate) | copy-start | bytes 4612
  88.2 17.8 %copy-start.6 = (bf16[256,16]{1,0:T(8,128)(2,1)}, bf16[256,16]{1,0:T(8,128)(2,1)S(1)}, u32[]{:S(2)}) copy-start(bf16[256,16]{1,0:T(8,128)(2,1)S(1)} %pad.5.member) | copy-start | bytes 24580
  88.2 18.6 %copy-start.22 = (s32[2,128]{1,0:T(2,128)}, s32[2,128]{1,0:T(2,128)S(1)}, u32[]{:S(2)}) copy-start(s32[2,128]{1,0:T(2,128)S(1)} %get-tuple-element.163.self_row) | copy-start | bytes 3076
  88.4 18.5 %copy-start.8 = (s32[256,1]{1,0:T(8,128)}, s32[256,1]{1,0:T(8,128)S(1)}, u32[]{:S(2)}) copy-start(s32[256,1]{1,0:T(8,128)S(1)} %copy.57.segment) | copy-start | bytes 3076
  89.1 16.9 %copy-start.4 = (f32[256,384]{1,0:T(8,128)}, f32[256,384]{1,0:T(8,128)S(1)}, u32[]{:S(2)}) copy-start(f32[256,384]{1,0:T(8,128)S(1)} %copy.54.cosine) | copy-start | bytes 1179652
  89.3 16.6 %copy-start.5 = (f32[256,384]{1,0:T(8,128)}, f32[256,384]{1,0:T(8,128)S(1)}, u32[]{:S(2)}) copy-start(f32[256,384]{1,0:T(8,128)S(1)} %copy.55.sine) | copy-start | bytes 1179652
  89.4 17.5 %copy-start.24 = (bf16[12,256,384]{2,1,0:T(8,128)(2,1)S(1)}, bf16[12,256,384]{2,1,0:T(8,128)(2,1)}, u32[]{:S(2)}) copy-start(bf16[12,256,384]{2,1,0:T(8,128)(2,1)} %get-tuple-element.92.text_key_far) | copy-start | bytes 7077892
  106.7 8.3 %copy-start.25 = (bf16[256,1536]{1,0:T(8,128)(2,1)}, bf16[256,1536]{1,0:T(8,128)(2,1)S(1)}, u32[]{:S(2)}) copy-start(bf16[256,1536]{1,0:T(8,128)(2,1)S(1)} %get-tuple-element.103.attn_in) | copy-start | bytes 2359300
  106.7 8.3 %copy-start.29 = (f32[256,384]{1,0:T(8,128)}, f32[256,384]{1,0:T(8,128)S(1)}, u32[]{:S(2)}) copy-start(f32[256,384]{1,0:T(8,128)S(1)} %get-tuple-element.100.key_raw) | copy-start | bytes 1179652
  106.7 8.3 %copy-start.30 = (bf16[256,384]{1,0:T(8,128)(2,1)}, bf16[256,384]{1,0:T(8,128)(2,1)S(1)}, u32[]{:S(2)}) copy-start(bf16[256,384]{1,0:T(8,128)(2,1)S(1)} %get-tuple-element.89.query) | copy-start | bytes 589828
  106.7 8.3 %copy-start.31 = (bf16[256,384]{1,0:T(8,128)(2,1)}, bf16[256,384]{1,0:T(8,128)(2,1)S(1)}, u32[]{:S(2)}) copy-start(bf16[256,384]{1,0:T(8,128)(2,1)S(1)} %get-tuple-element.90.key) | copy-start | bytes 589828
  106.7 8.3 %copy-start.32 = (bf16[256,384]{1,0:T(8,128)(2,1)}, bf16[256,384]{1,0:T(8,128)(2,1)S(1)}, u32[]{:S(2)}) copy-start(bf16[256,384]{1,0:T(8,128)(2,1)S(1)} %get-tuple-element.91.value) | copy-start | bytes 589828
  106.8 8.3 %copy-start.35 = (s32[12]{0:T(128)}, s32[12]{0:T(128)S(1)}, u32[]{:S(2)}) copy-start(s32[12]{0:T(128)S(1)} %or_convert_fusion.live) | copy-start | bytes 148
  106.8 8.3 %copy-start.12 = (s32[256,1]{1,0:T(8,128)}, s32[256,1]{1,0:T(8,128)S(1)}, u32[]{:S(2)}) copy-start(s32[256,1]{1,0:T(8,128)S(1)} %bitcast_select_fusion.self_id) | copy-start | bytes 3076
  220.3 16.7 %copy-start.26 = (bf16[256,1536]{1,0:T(8,128)(2,1)S(1)}, bf16[256,1536]{1,0:T(8,128)(2,1)}, u32[]{:S(2)}) copy-start(bf16[256,1536]{1,0:T(8,128)(2,1)} %copy-done.25) | copy-start | bytes 2359300
  220.3 16.7 %copy-start.27 = (bf16[256,1536]{1,0:T(8,128)(2,1)S(1)}, bf16[256,1536]{1,0:T(8,128)(2,1)}, u32[]{:S(2)}) copy-start(bf16[256,1536]{1,0:T(8,128)(2,1)} %get-tuple-element.107.grad_out) | copy-start | bytes 2359300
  320.4 5.7 %copy-start.49 = (f32[1,192]{1,0:T(1,128)S(1)}, f32[1,192]{1,0:T(1,128)}, u32[]{:S(2)}) copy-start(f32[1,192]{1,0:T(1,128)} %get-tuple-element.140) | copy-start | bytes 2308
  320.4 6.3 %copy-start.48 = (f32[1,192]{1,0:T(1,128)S(1)}, f32[1,192]{1,0:T(1,128)}, u32[]{:S(2)}) copy-start(f32[1,192]{1,0:T(1,128)} %get-tuple-element.141) | copy-start | bytes 2308
  320.4 6.8 %copy-start.47 = (f32[8,6]{1,0:T(8,128)S(1)}, f32[8,6]{1,0:T(8,128)}, u32[]{:S(2)}) copy-start(f32[8,6]{1,0:T(8,128)} %get-tuple-element.207) | copy-start | bytes 580
  320.4 7.4 %copy-start.46 = (f32[8,6]{1,0:T(8,128)S(1)}, f32[8,6]{1,0:T(8,128)}, u32[]{:S(2)}) copy-start(f32[8,6]{1,0:T(8,128)} %get-tuple-element.208) | copy-start | bytes 580
  320.4 8.0 %copy-start.45 = (f32[8,6]{1,0:T(8,128)S(1)}, f32[8,6]{1,0:T(8,128)}, u32[]{:S(2)}) copy-start(f32[8,6]{1,0:T(8,128)} %get-tuple-element.209) | copy-start | bytes 580
  320.5 8.6 %copy-start.52 = (f32[1,6]{1,0:T(1,128)S(1)}, f32[1,6]{1,0:T(1,128)}, u32[]{:S(2)}) copy-start(f32[1,6]{1,0:T(1,128)} %get-tuple-element.145) | copy-start | bytes 76
  (22 other events, 56.9 us)
Sparse Core Ops, SparseCore 0:
  86.6 58.4 all-gather.1

commit v2 on v1

--- a/solution.py
+++ b/solution.py
@@ -1600,6 +1600,7 @@
         ],
         flops=14 * rows * width * local,
         traffic=15 * 2**20,
+        vmem=62,
     )
     depth = DT // parts
     caption_rows = captions.reshape(images * TXT, DT)

time: 343 us -> 342 us (level)
  local copies, waits for them, and re-layouts: 17.8 us -> 13.4 us
  Pallas kernels: 300 us -> 304 us
    pallas_call x4, Pallas kernels: 47.8 us -> 56.2 us  [run(): pl.pallas_call(body, out_shape=outs, in_specs=[pl.BlockSpec(memory_space=...]
    pallas_call x4, Pallas kernels: 246 us -> 242 us  [exchange(): pl.pallas_call(body, out_shape=[shape for shape, _ in outs], in_specs=[pl...]
    unnamed x117 -> x105, local copies, waits for them, and re-layouts: 15.2 us -> 10.7 us
  transfers between devices with their start and end apart: 1 -> 1, of which waited for: 0 -> 0; matrix products, arithmetic and copies ran while one was open for 1% -> 1% of each run, Pallas kernels for 19% -> 20%
where the time goes in v2:
time: 342 us; the launch traced here: 336 us
  Pallas kernels  304 us (89%)
  between operations  15 us (4%)
  local copies, waits for them, and re-layouts  13.4 us (4%)
  other arithmetic  3.82 us (1%)
    pallas_call x4, Pallas kernels, exchange(): pl.pallas_call(body, out_shape=[shape for shape, _ in outs], in_specs=[pl...  242 us
    pallas_call x4, Pallas kernels, run(): pl.pallas_call(body, out_shape=outs, in_specs=[pl.BlockSpec(memory_space=...  56.2 us
    unnamed x105, local copies, waits for them, and re-layouts  10.7 us
  transfers between devices with their start and end apart: 1, of which 0 were waited for; matrix products, arithmetic and copies ran while one was open for 1% of the time, Pallas kernels for 20%

profile of v2, /device:TPU:8, one launch (start us, length us, event | category | flops | bytes accessed | tf_op | source)
XLA Modules:
  0.0 335.8 jit_solution(18271040115918918822)
XLA Ops:
  7.3 0.9 broadcast_in_dim.30.attn_own
  8.2 0.7 broadcast_in_dim.31.ffn_own
  8.9 0.7 copy.53.context
  9.6 2.4 pad_maximum_fusion
  12.2 71.0 %shard_map.349 = (bf16[12,256,384]{2,1,0:T(8,128)(2,1)S(1)}, bf16[12,256,384]{2,1,0:T(8,128)(2,1)}, bf16[12,256,384]{2,1,0:T(8,128)(2,1)}, bf16[1536,768]{1,0:T(...) custom-call(bf16[512,384]{1,0:T(8,128)(2,1)S(1)} %copy-done.7, ...), custom_call_target="tpu_custom_call" | custom-call | tf_op jit(solution)/shard_map/pallas_call | solution.py:611
  83.2 0.6 copy-done.11
  83.8 0.6 copy-done.13
  84.4 1.4 copy-done.21
  85.8 0.6 copy-done.29
  86.7 0.2 reduce-window.14
  86.9 0.2 reduce-window.15
  87.8 0.2 copy.64
  88.9 0.2 copy.54.cosine
  89.2 0.2 copy.55.sine
  89.4 16.5 %shard_map.350 = (bf16[256,1536]{1,0:T(8,128)(2,1)S(1)}, f32[256,384]{1,0:T(8,128)S(1)}, f32[256,384]{1,0:T(8,128)S(1)}, bf16[256,384]{1,0:T(8,128)(2,1)S(1)}, b...) custom-call(bf16[256,1536]{1,0:T(8,128)(2,1)S(1)} %bitcast.100, bf16[256,16]{1,0:T(8,128)(2,1)S(1)} %pad.5.member, ...), custom_call_target="tpu_custom_call" | custom-call | flops 905969664 | bytes 10485760 | tf_op jit(solution)/shard_map/pallas_call | solution.py:70
  106.0 0.7 copy-done.24
  106.9 10.8 %shard_map.351 = (bf16[256,384]{1,0:T(8,128)(2,1)S(1)}, f32[256,384]{1,0:T(8,128)S(1)}, bf16[256,1536]{1,0:T(8,128)(2,1)S(1)}) custom-call(s32[12]{0:T(128)S(1)} %or_convert_fusion.live, s32[12]{0:T(128)S(1)} %reshape.690.text_len, bf16[256,384]{1,0:T(8,128)(2,1)S(1)} %get-tuple-element.89.query, bf16[256,384]{1,0:T(8,128)(2,1)S(1)} %get-tuple-element.90.key, ...), custom_call_target="tpu_custom_call" | custom-call | flops 2147483648 | bytes 12582912 | tf_op jit(solution)/shard_map/pallas_call | solution.py:70
  117.7 0.7 copy-done.32
  118.5 0.7 copy-done.33
  119.1 39.1 %shard_map.352.attn_out.attn_far = bf16[256,1536]{1,0:T(8,128)(2,1)S(1)} custom-call(bf16[256,1536]{1,0:T(8,128)(2,1)S(1)} %get-tuple-element.94.partial), custom_call_target="tpu_custom_call" | custom-call | tf_op jit(solution)/shard_map/pallas_call | solution.py:611
  158.2 0.9 copy-done
  159.1 65.3 %shard_map.353 = (f32[256,1536]{1,0:T(8,128)}, f32[256,1536]{1,0:T(8,128)}, bf16[256,1536]{1,0:T(8,128)(2,1)}, f32[256,384]{1,0:T(8,128)}, bf16[64,1536]{1,0:T(8...) custom-call(bf16[256,1536]{1,0:T(8,128)(2,1)} %bitcast.98, ...), custom_call_target="tpu_custom_call" | custom-call | tf_op jit(solution)/shard_map/pallas_call | solution.py:611
  224.4 20.5 %shard_map.354 = (bf16[256,384]{1,0:T(8,128)(2,1)}, bf16[256,384]{1,0:T(8,128)(2,1)}, bf16[256,384]{1,0:T(8,128)(2,1)}, bf16[768,3072]{1,0:T(8,128)(2,1)}, f32[8,384]{1,0:T(8,128)}) custom-call(s32[12]{0:T(128)} %copy-done.31, s32[12]{0:T(128)} %copy-done.30, f32[256,384]{1,0:T(8,128)} %get-tuple-element.96.grad_mixed, f32[256,384]{1,0:T(8,128)} %copy-done.32, ...), custom_call_target="tpu_custom_call" | custom-call | flops 4294967296 | bytes 15728640 | tf_op jit(solution)/shard_map/pallas_call | solution.py:70
  244.9 8.4 %shard_map.355 = (bf16[1536,768]{1,0:T(8,128)(2,1)}, bf16[1536,768]{1,0:T(8,128)(2,1)}, bf16[256,1536]{1,0:T(8,128)(2,1)}) custom-call(bf16[256,1536]{1,0:T(8,128)(2,1)} %copy-done.23, bf16[256,384]{1,0:T(8,128)(2,1)} %get-tuple-element.104.grad_query, bf16[256,384]{1,0:T(8,128)(2,1)} %get-tuple-element.105.grad_key, ...), custom_call_target="tpu_custom_call" | custom-call | flops 2113929216 | bytes 15728640 | tf_op jit(solution)/shard_map/pallas_call | solution.py:70
  253.3 66.4 %shard_map.356 = (f32[192,768]{1,0:T(8,128)}, f32[192,768]{1,0:T(8,128)}, f32[768,512]{1,0:T(8,128)}, bf16[256,1536]{1,0:T(8,128)(2,1)}, bf16[256,1536]{1,0:T(8,...) custom-call(bf16[3072,4096]{1,0:T(8,128)(2,1)} %bitcast.102, ...), custom_call_target="tpu_custom_call" | custom-call | tf_op jit(solution)/shard_map/pallas_call | solution.py:611
  319.7 5.6 %shard_map.357 = (f32[192,384]{1,0:T(8,128)}, f32[192,384]{1,0:T(8,128)}, f32[192,384]{1,0:T(8,128)}, f32[192,384]{1,0:T(8,128)}, f32[512,384]{1,0:T(8,128)}, /*...) custom-call(f32[192,768]{1,0:T(8,128)} %get-tuple-element.119.refs_0, ...), custom_call_target="tpu_custom_call" | custom-call | tf_op jit(solution)/shard_map/pallas_call | solution.py:1700
  325.4 0.6 copy.73
  325.9 0.6 copy.74
  326.5 0.6 copy.75
  327.1 0.6 copy.76
  327.7 0.6 copy.77
  328.3 0.5 copy.78
  (131 shorter events, 2.1 us)
Async XLA Ops:
  7.2 4.8 %copy-start.16 = (bf16[8,6]{1,0:T(8,128)(2,1)S(1)}, bf16[8,6]{1,0:T(8,128)(2,1)}, u32[]{:S(2)}) copy-start(bf16[8,6]{1,0:T(8,128)(2,1)} %t_own.1) | copy-start | bytes 292
  7.2 4.8 %copy-start.15 = (bf16[8,6]{1,0:T(8,128)(2,1)S(1)}, bf16[8,6]{1,0:T(8,128)(2,1)}, u32[]{:S(2)}) copy-start(bf16[8,6]{1,0:T(8,128)(2,1)} %k_own.1) | copy-start | bytes 292
  7.3 4.8 %copy-start.14 = (bf16[8,6]{1,0:T(8,128)(2,1)S(1)}, bf16[8,6]{1,0:T(8,128)(2,1)}, u32[]{:S(2)}) copy-start(bf16[8,6]{1,0:T(8,128)(2,1)} %q_own.1) | copy-start | bytes 292
  7.3 151.8 %all-gather.2.cloned.1.call-start = ((), (), s32[]{:S(2)}) async-start(), calls=%async_computation | async-start | bytes 10616832 | tf_op jit(solution)/shard_map/all_gather | solution.py:1320
  12.1 74.3 %copy-start.44 = (s32[2,6]{1,0:T(2,128)S(1)}, s32[2,6]{1,0:T(2,128)}, u32[]{:S(2)}) copy-start(s32[2,6]{1,0:T(2,128)} %param.26) | copy-start | bytes 148
  12.1 74.4 %copy-start.38 = (s32[2,6,2]{1,2,0:T(2,128)S(1)}, s32[2,6,2]{1,2,0:T(2,128)}, u32[]{:S(2)}) copy-start(s32[2,6,2]{1,2,0:T(2,128)} %param.25) | copy-start | bytes 292
  12.2 75.5 %copy-start.45 = (bf16[6]{0:T(256)(128)(2,1)S(1)}, bf16[6]{0:T(256)(128)(2,1)}, u32[]{:S(2)}) copy-start(bf16[6]{0:T(256)(128)(2,1)} %param.42) | copy-start | bytes 40
  86.4 19.5 %copy-start.2 = (bf16[4,16,1536]{2,1,0:T(8,128)(2,1)}, bf16[4,16,1536]{2,1,0:T(8,128)(2,1)S(1)}, u32[]{:S(2)}) copy-start(bf16[4,16,1536]{2,1,0:T(8,128)(2,1)S(1)} %get-tuple-element.83.mods) | copy-start | bytes 589828
  86.4 19.5 %copy-start.12 = (f32[1,1536]{1,0:T(1,128)}, f32[1,1536]{1,0:T(1,128)S(1)}, u32[]{:S(2)}) copy-start(f32[1,1536]{1,0:T(1,128)S(1)} %get-tuple-element.84.gain.attn_gain) | copy-start | bytes 18436
  86.4 19.6 %copy-start.17 = (f32[1,384]{1,0:T(1,128)}, f32[1,384]{1,0:T(1,128)S(1)}, u32[]{:S(2)}) copy-start(f32[1,384]{1,0:T(1,128)S(1)} %get-tuple-element.85.q_gain) | copy-start | bytes 4612
  86.4 19.6 %copy-start.18 = (f32[1,384]{1,0:T(1,128)}, f32[1,384]{1,0:T(1,128)S(1)}, u32[]{:S(2)}) copy-start(f32[1,384]{1,0:T(1,128)S(1)} %get-tuple-element.86.k_gain) | copy-start | bytes 4612
  86.5 20.3 %copy-start.30 = (s32[12]{0:T(128)}, s32[12]{0:T(128)S(1)}, u32[]{:S(2)}) copy-start(s32[12]{0:T(128)S(1)} %reshape.690.text_len) | copy-start | bytes 148
  87.8 19.0 %copy-start.19 = (f32[1,384]{1,0:T(1,128)}, f32[1,384]{1,0:T(1,128)S(1)}, u32[]{:S(2)}) copy-start(f32[1,384]{1,0:T(1,128)S(1)} %broadcast_in_dim_reshape.3.gate) | copy-start | bytes 4612
  88.2 17.8 %copy-start.5 = (bf16[256,16]{1,0:T(8,128)(2,1)}, bf16[256,16]{1,0:T(8,128)(2,1)S(1)}, u32[]{:S(2)}) copy-start(bf16[256,16]{1,0:T(8,128)(2,1)S(1)} %pad.5.member) | copy-start | bytes 24580
  88.2 18.6 %copy-start.20 = (s32[2,128]{1,0:T(2,128)}, s32[2,128]{1,0:T(2,128)S(1)}, u32[]{:S(2)}) copy-start(s32[2,128]{1,0:T(2,128)S(1)} %get-tuple-element.163.self_row) | copy-start | bytes 3076
  88.3 18.5 %copy-start.6 = (s32[256,1]{1,0:T(8,128)}, s32[256,1]{1,0:T(8,128)S(1)}, u32[]{:S(2)}) copy-start(s32[256,1]{1,0:T(8,128)S(1)} %copy.57.segment) | copy-start | bytes 3076
  89.1 16.9 %copy-start.3 = (f32[256,384]{1,0:T(8,128)}, f32[256,384]{1,0:T(8,128)S(1)}, u32[]{:S(2)}) copy-start(f32[256,384]{1,0:T(8,128)S(1)} %copy.54.cosine) | copy-start | bytes 1179652
  89.3 16.6 %copy-start.4 = (f32[256,384]{1,0:T(8,128)}, f32[256,384]{1,0:T(8,128)S(1)}, u32[]{:S(2)}) copy-start(f32[256,384]{1,0:T(8,128)S(1)} %copy.55.sine) | copy-start | bytes 1179652
  89.3 17.5 %copy-start.22 = (bf16[12,256,384]{2,1,0:T(8,128)(2,1)S(1)}, bf16[12,256,384]{2,1,0:T(8,128)(2,1)}, u32[]{:S(2)}) copy-start(bf16[12,256,384]{2,1,0:T(8,128)(2,1)} %get-tuple-element.92.text_key_far) | copy-start | bytes 7077892
  106.7 10.9 %copy-start.23 = (bf16[256,1536]{1,0:T(8,128)(2,1)}, bf16[256,1536]{1,0:T(8,128)(2,1)S(1)}, u32[]{:S(2)}) copy-start(bf16[256,1536]{1,0:T(8,128)(2,1)S(1)} %get-tuple-element.103.attn_in) | copy-start | bytes 2359300
  106.7 10.9 %copy-start.25 = (f32[256,384]{1,0:T(8,128)}, f32[256,384]{1,0:T(8,128)S(1)}, u32[]{:S(2)}) copy-start(f32[256,384]{1,0:T(8,128)S(1)} %get-tuple-element.100.key_raw) | copy-start | bytes 1179652
  106.7 10.9 %copy-start.26 = (bf16[256,384]{1,0:T(8,128)(2,1)}, bf16[256,384]{1,0:T(8,128)(2,1)S(1)}, u32[]{:S(2)}) copy-start(bf16[256,384]{1,0:T(8,128)(2,1)S(1)} %get-tuple-element.89.query) | copy-start | bytes 589828
  106.7 10.9 %copy-start.27 = (bf16[256,384]{1,0:T(8,128)(2,1)}, bf16[256,384]{1,0:T(8,128)(2,1)S(1)}, u32[]{:S(2)}) copy-start(bf16[256,384]{1,0:T(8,128)(2,1)S(1)} %get-tuple-element.90.key) | copy-start | bytes 589828
  106.7 11.0 %copy-start.28 = (bf16[256,384]{1,0:T(8,128)(2,1)}, bf16[256,384]{1,0:T(8,128)(2,1)S(1)}, u32[]{:S(2)}) copy-start(bf16[256,384]{1,0:T(8,128)(2,1)S(1)} %get-tuple-element.91.value) | copy-start | bytes 589828
  106.8 10.9 %copy-start.31 = (s32[12]{0:T(128)}, s32[12]{0:T(128)S(1)}, u32[]{:S(2)}) copy-start(s32[12]{0:T(128)S(1)} %or_convert_fusion.live) | copy-start | bytes 148
  106.8 10.9 %copy-start.10 = (s32[256,1]{1,0:T(8,128)}, s32[256,1]{1,0:T(8,128)S(1)}, u32[]{:S(2)}) copy-start(s32[256,1]{1,0:T(8,128)S(1)} %bitcast_select_fusion.self_id) | copy-start | bytes 3076
  319.6 5.7 %copy-start.43 = (f32[1,192]{1,0:T(1,128)S(1)}, f32[1,192]{1,0:T(1,128)}, u32[]{:S(2)}) copy-start(f32[1,192]{1,0:T(1,128)} %get-tuple-element.140) | copy-start | bytes 2308
  319.7 6.3 %copy-start.42 = (f32[1,192]{1,0:T(1,128)S(1)}, f32[1,192]{1,0:T(1,128)}, u32[]{:S(2)}) copy-start(f32[1,192]{1,0:T(1,128)} %get-tuple-element.141) | copy-start | bytes 2308
  319.7 6.8 %copy-start.41 = (f32[8,6]{1,0:T(8,128)S(1)}, f32[8,6]{1,0:T(8,128)}, u32[]{:S(2)}) copy-start(f32[8,6]{1,0:T(8,128)} %get-tuple-element.207) | copy-start | bytes 580
  319.7 7.4 %copy-start.40 = (f32[8,6]{1,0:T(8,128)S(1)}, f32[8,6]{1,0:T(8,128)}, u32[]{:S(2)}) copy-start(f32[8,6]{1,0:T(8,128)} %get-tuple-element.208) | copy-start | bytes 580
  319.7 8.0 %copy-start.39 = (f32[8,6]{1,0:T(8,128)S(1)}, f32[8,6]{1,0:T(8,128)}, u32[]{:S(2)}) copy-start(f32[8,6]{1,0:T(8,128)} %get-tuple-element.209) | copy-start | bytes 580
  319.7 8.6 %copy-start.46 = (f32[1,6]{1,0:T(1,128)S(1)}, f32[1,6]{1,0:T(1,128)}, u32[]{:S(2)}) copy-start(f32[1,6]{1,0:T(1,128)} %get-tuple-element.145) | copy-start | bytes 76
  (16 other events, 42.8 us)
Sparse Core Ops, SparseCore 0:
  86.5 58.5 all-gather.1

commit v3 on v2

--- a/solution.py
+++ b/solution.py
@@ -1130,14 +1130,15 @@
     for piece in (3, 2, 1, 0):
         for number in range(2):
             reduces[number].second(piece, firsts[number][piece])
-    work(2, 4)
+    work(2, 3)
+    sum_in.add(grad_in, True)
+    sum_in.gather(grad_in)
+    work(3, 4)
     text_firsts = {}
     for piece in (3, 2, 1, 0):
         text_firsts[piece] = text.first(piece, text_total.at[2 * piece + 1])
     text_firsts[1].start()
     text_firsts[0].start()
-    sum_in.add(grad_in, True)
-    sum_in.gather(grad_in)
     for reduce in reduces:
         reduce.third()
     work(4, 5)

time: 342 us -> 344 us (level); the launches traced: 336 us -> 343 us
  Pallas kernels: 304 us -> 311 us
    pallas_call x4, Pallas kernels: 242 us -> 252 us  [exchange(): pl.pallas_call(body, out_shape=[shape for shape, _ in outs], in_specs=[pl...]
  transfers between devices with their start and end apart: 1 -> 1, of which waited for: 0 -> 0; matrix products, arithmetic and copies ran while one was open for 1% -> 1% of each run, Pallas kernels for 20% -> 18%
where the time goes in v3:
time: 344 us; the launch traced here: 343 us
  Pallas kernels  311 us (90%)
  between operations  15 us (4%)
  local copies, waits for them, and re-layouts  13.4 us (4%)
  other arithmetic  3.82 us (1%)
    pallas_call x4, Pallas kernels, exchange(): pl.pallas_call(body, out_shape=[shape for shape, _ in outs], in_specs=[pl...  252 us
    pallas_call x4, Pallas kernels, run(): pl.pallas_call(body, out_shape=outs, in_specs=[pl.BlockSpec(memory_space=...  52.9 us
    unnamed x105, local copies, waits for them, and re-layouts  10.7 us
  transfers between devices with their start and end apart: 1, of which 0 were waited for; matrix products, arithmetic and copies ran while one was open for 1% of the time, Pallas kernels for 18%

profile of v3, /device:TPU:8, one launch (start us, length us, event | category | flops | bytes accessed | tf_op | source)
XLA Modules:
  0.0 343.3 jit_solution(18056423001285990008)
XLA Ops:
  7.3 0.9 broadcast_in_dim.30.attn_own
  8.2 0.7 broadcast_in_dim.31.ffn_own
  8.9 0.7 copy.53.context
  9.6 2.4 pad_maximum_fusion
  12.2 71.0 %shard_map.349 = (bf16[12,256,384]{2,1,0:T(8,128)(2,1)S(1)}, bf16[12,256,384]{2,1,0:T(8,128)(2,1)}, bf16[12,256,384]{2,1,0:T(8,128)(2,1)}, bf16[1536,768]{1,0:T(...) custom-call(bf16[512,384]{1,0:T(8,128)(2,1)S(1)} %copy-done.7, ...), custom_call_target="tpu_custom_call" | custom-call | tf_op jit(solution)/shard_map/pallas_call | solution.py:611
  83.2 0.6 copy-done.11
  83.8 0.6 copy-done.13
  84.4 1.4 copy-done.21
  85.8 0.6 copy-done.29
  86.7 0.2 reduce-window.14
  86.9 0.2 reduce-window.15
  87.8 0.2 copy.64
  88.9 0.2 copy.54.cosine
  89.2 0.2 copy.55.sine
  89.4 16.5 %shard_map.350 = (bf16[256,1536]{1,0:T(8,128)(2,1)S(1)}, f32[256,384]{1,0:T(8,128)S(1)}, f32[256,384]{1,0:T(8,128)S(1)}, bf16[256,384]{1,0:T(8,128)(2,1)S(1)}, b...) custom-call(bf16[256,1536]{1,0:T(8,128)(2,1)S(1)} %bitcast.100, bf16[256,16]{1,0:T(8,128)(2,1)S(1)} %pad.5.member, ...), custom_call_target="tpu_custom_call" | custom-call | flops 905969664 | bytes 10485760 | tf_op jit(solution)/shard_map/pallas_call | solution.py:70
  106.0 0.7 copy-done.24
  106.9 9.5 %shard_map.351 = (bf16[256,384]{1,0:T(8,128)(2,1)S(1)}, f32[256,384]{1,0:T(8,128)S(1)}, bf16[256,1536]{1,0:T(8,128)(2,1)S(1)}) custom-call(s32[12]{0:T(128)S(1)} %or_convert_fusion.live, s32[12]{0:T(128)S(1)} %reshape.690.text_len, bf16[256,384]{1,0:T(8,128)(2,1)S(1)} %get-tuple-element.89.query, bf16[256,384]{1,0:T(8,128)(2,1)S(1)} %get-tuple-element.90.key, ...), custom_call_target="tpu_custom_call" | custom-call | flops 2147483648 | bytes 12582912 | tf_op jit(solution)/shard_map/pallas_call | solution.py:70
  116.4 0.7 copy-done.32
  117.1 0.7 copy-done.33
  117.8 37.4 %shard_map.352.attn_out.attn_far = bf16[256,1536]{1,0:T(8,128)(2,1)S(1)} custom-call(bf16[256,1536]{1,0:T(8,128)(2,1)S(1)} %get-tuple-element.94.partial), custom_call_target="tpu_custom_call" | custom-call | tf_op jit(solution)/shard_map/pallas_call | solution.py:611
  155.3 0.9 copy-done
  156.1 64.2 %shard_map.353 = (f32[256,1536]{1,0:T(8,128)}, f32[256,1536]{1,0:T(8,128)}, bf16[256,1536]{1,0:T(8,128)(2,1)}, f32[256,384]{1,0:T(8,128)}, bf16[64,1536]{1,0:T(8...) custom-call(bf16[256,1536]{1,0:T(8,128)(2,1)} %bitcast.98, ...), custom_call_target="tpu_custom_call" | custom-call | tf_op jit(solution)/shard_map/pallas_call | solution.py:611
  220.3 18.5 %shard_map.354 = (bf16[256,384]{1,0:T(8,128)(2,1)}, bf16[256,384]{1,0:T(8,128)(2,1)}, bf16[256,384]{1,0:T(8,128)(2,1)}, bf16[768,3072]{1,0:T(8,128)(2,1)}, f32[8,384]{1,0:T(8,128)}) custom-call(s32[12]{0:T(128)} %copy-done.31, s32[12]{0:T(128)} %copy-done.30, f32[256,384]{1,0:T(8,128)} %get-tuple-element.96.grad_mixed, f32[256,384]{1,0:T(8,128)} %copy-done.32, ...), custom_call_target="tpu_custom_call" | custom-call | flops 4294967296 | bytes 15728640 | tf_op jit(solution)/shard_map/pallas_call | solution.py:70
  238.9 8.4 %shard_map.355 = (bf16[1536,768]{1,0:T(8,128)(2,1)}, bf16[1536,768]{1,0:T(8,128)(2,1)}, bf16[256,1536]{1,0:T(8,128)(2,1)}) custom-call(bf16[256,1536]{1,0:T(8,128)(2,1)} %copy-done.23, bf16[256,384]{1,0:T(8,128)(2,1)} %get-tuple-element.104.grad_query, bf16[256,384]{1,0:T(8,128)(2,1)} %get-tuple-element.105.grad_key, ...), custom_call_target="tpu_custom_call" | custom-call | flops 2113929216 | bytes 15728640 | tf_op jit(solution)/shard_map/pallas_call | solution.py:70
  247.2 79.8 %shard_map.356 = (f32[192,768]{1,0:T(8,128)}, f32[192,768]{1,0:T(8,128)}, f32[768,512]{1,0:T(8,128)}, bf16[256,1536]{1,0:T(8,128)(2,1)}, bf16[256,1536]{1,0:T(8,...) custom-call(bf16[3072,4096]{1,0:T(8,128)(2,1)} %bitcast.102, ...), custom_call_target="tpu_custom_call" | custom-call | tf_op jit(solution)/shard_map/pallas_call | solution.py:611
  327.1 5.6 %shard_map.357 = (f32[192,384]{1,0:T(8,128)}, f32[192,384]{1,0:T(8,128)}, f32[192,384]{1,0:T(8,128)}, f32[192,384]{1,0:T(8,128)}, f32[512,384]{1,0:T(8,128)}, /*...) custom-call(f32[192,768]{1,0:T(8,128)} %get-tuple-element.119.refs_0, ...), custom_call_target="tpu_custom_call" | custom-call | tf_op jit(solution)/shard_map/pallas_call | solution.py:1701
  332.8 0.6 copy.73
  333.4 0.6 copy.74
  333.9 0.6 copy.75
  334.5 0.6 copy.76
  335.1 0.6 copy.77
  335.7 0.5 copy.78
  (131 shorter events, 2.1 us)
Async XLA Ops:
  7.2 4.8 %copy-start.16 = (bf16[8,6]{1,0:T(8,128)(2,1)S(1)}, bf16[8,6]{1,0:T(8,128)(2,1)}, u32[]{:S(2)}) copy-start(bf16[8,6]{1,0:T(8,128)(2,1)} %t_own.1) | copy-start | bytes 292
  7.2 4.8 %copy-start.15 = (bf16[8,6]{1,0:T(8,128)(2,1)S(1)}, bf16[8,6]{1,0:T(8,128)(2,1)}, u32[]{:S(2)}) copy-start(bf16[8,6]{1,0:T(8,128)(2,1)} %k_own.1) | copy-start | bytes 292
  7.3 4.8 %copy-start.14 = (bf16[8,6]{1,0:T(8,128)(2,1)S(1)}, bf16[8,6]{1,0:T(8,128)(2,1)}, u32[]{:S(2)}) copy-start(bf16[8,6]{1,0:T(8,128)(2,1)} %q_own.1) | copy-start | bytes 292
  7.3 148.8 %all-gather.2.cloned.1.call-start = ((), (), s32[]{:S(2)}) async-start(), calls=%async_computation | async-start | bytes 10616832 | tf_op jit(solution)/shard_map/all_gather | solution.py:1321
  12.1 74.3 %copy-start.44 = (s32[2,6]{1,0:T(2,128)S(1)}, s32[2,6]{1,0:T(2,128)}, u32[]{:S(2)}) copy-start(s32[2,6]{1,0:T(2,128)} %param.26) | copy-start | bytes 148
  12.1 74.4 %copy-start.38 = (s32[2,6,2]{1,2,0:T(2,128)S(1)}, s32[2,6,2]{1,2,0:T(2,128)}, u32[]{:S(2)}) copy-start(s32[2,6,2]{1,2,0:T(2,128)} %param.25) | copy-start | bytes 292
  12.2 75.5 %copy-start.45 = (bf16[6]{0:T(256)(128)(2,1)S(1)}, bf16[6]{0:T(256)(128)(2,1)}, u32[]{:S(2)}) copy-start(bf16[6]{0:T(256)(128)(2,1)} %param.42) | copy-start | bytes 40
  86.4 19.5 %copy-start.2 = (bf16[4,16,1536]{2,1,0:T(8,128)(2,1)}, bf16[4,16,1536]{2,1,0:T(8,128)(2,1)S(1)}, u32[]{:S(2)}) copy-start(bf16[4,16,1536]{2,1,0:T(8,128)(2,1)S(1)} %get-tuple-element.83.mods) | copy-start | bytes 589828
  86.4 19.5 %copy-start.12 = (f32[1,1536]{1,0:T(1,128)}, f32[1,1536]{1,0:T(1,128)S(1)}, u32[]{:S(2)}) copy-start(f32[1,1536]{1,0:T(1,128)S(1)} %get-tuple-element.84.gain.attn_gain) | copy-start | bytes 18436
  86.4 19.6 %copy-start.17 = (f32[1,384]{1,0:T(1,128)}, f32[1,384]{1,0:T(1,128)S(1)}, u32[]{:S(2)}) copy-start(f32[1,384]{1,0:T(1,128)S(1)} %get-tuple-element.85.q_gain) | copy-start | bytes 4612
  86.4 19.6 %copy-start.18 = (f32[1,384]{1,0:T(1,128)}, f32[1,384]{1,0:T(1,128)S(1)}, u32[]{:S(2)}) copy-start(f32[1,384]{1,0:T(1,128)S(1)} %get-tuple-element.86.k_gain) | copy-start | bytes 4612
  86.5 20.3 %copy-start.30 = (s32[12]{0:T(128)}, s32[12]{0:T(128)S(1)}, u32[]{:S(2)}) copy-start(s32[12]{0:T(128)S(1)} %reshape.690.text_len) | copy-start | bytes 148
  87.8 19.0 %copy-start.19 = (f32[1,384]{1,0:T(1,128)}, f32[1,384]{1,0:T(1,128)S(1)}, u32[]{:S(2)}) copy-start(f32[1,384]{1,0:T(1,128)S(1)} %broadcast_in_dim_reshape.3.gate) | copy-start | bytes 4612
  88.2 17.8 %copy-start.5 = (bf16[256,16]{1,0:T(8,128)(2,1)}, bf16[256,16]{1,0:T(8,128)(2,1)S(1)}, u32[]{:S(2)}) copy-start(bf16[256,16]{1,0:T(8,128)(2,1)S(1)} %pad.5.member) | copy-start | bytes 24580
  88.2 18.6 %copy-start.20 = (s32[2,128]{1,0:T(2,128)}, s32[2,128]{1,0:T(2,128)S(1)}, u32[]{:S(2)}) copy-start(s32[2,128]{1,0:T(2,128)S(1)} %get-tuple-element.163.self_row) | copy-start | bytes 3076
  88.3 18.5 %copy-start.6 = (s32[256,1]{1,0:T(8,128)}, s32[256,1]{1,0:T(8,128)S(1)}, u32[]{:S(2)}) copy-start(s32[256,1]{1,0:T(8,128)S(1)} %copy.57.segment) | copy-start | bytes 3076
  89.1 16.9 %copy-start.3 = (f32[256,384]{1,0:T(8,128)}, f32[256,384]{1,0:T(8,128)S(1)}, u32[]{:S(2)}) copy-start(f32[256,384]{1,0:T(8,128)S(1)} %copy.54.cosine) | copy-start | bytes 1179652
  89.3 16.6 %copy-start.4 = (f32[256,384]{1,0:T(8,128)}, f32[256,384]{1,0:T(8,128)S(1)}, u32[]{:S(2)}) copy-start(f32[256,384]{1,0:T(8,128)S(1)} %copy.55.sine) | copy-start | bytes 1179652
  89.3 17.5 %copy-start.22 = (bf16[12,256,384]{2,1,0:T(8,128)(2,1)S(1)}, bf16[12,256,384]{2,1,0:T(8,128)(2,1)}, u32[]{:S(2)}) copy-start(bf16[12,256,384]{2,1,0:T(8,128)(2,1)} %get-tuple-element.92.text_key_far) | copy-start | bytes 7077892
  106.7 9.6 %copy-start.23 = (bf16[256,1536]{1,0:T(8,128)(2,1)}, bf16[256,1536]{1,0:T(8,128)(2,1)S(1)}, u32[]{:S(2)}) copy-start(bf16[256,1536]{1,0:T(8,128)(2,1)S(1)} %get-tuple-element.103.attn_in) | copy-start | bytes 2359300
  106.7 9.6 %copy-start.25 = (f32[256,384]{1,0:T(8,128)}, f32[256,384]{1,0:T(8,128)S(1)}, u32[]{:S(2)}) copy-start(f32[256,384]{1,0:T(8,128)S(1)} %get-tuple-element.100.key_raw) | copy-start | bytes 1179652
  106.7 9.6 %copy-start.26 = (bf16[256,384]{1,0:T(8,128)(2,1)}, bf16[256,384]{1,0:T(8,128)(2,1)S(1)}, u32[]{:S(2)}) copy-start(bf16[256,384]{1,0:T(8,128)(2,1)S(1)} %get-tuple-element.89.query) | copy-start | bytes 589828
  106.7 9.6 %copy-start.27 = (bf16[256,384]{1,0:T(8,128)(2,1)}, bf16[256,384]{1,0:T(8,128)(2,1)S(1)}, u32[]{:S(2)}) copy-start(bf16[256,384]{1,0:T(8,128)(2,1)S(1)} %get-tuple-element.90.key) | copy-start | bytes 589828
  106.7 9.6 %copy-start.28 = (bf16[256,384]{1,0:T(8,128)(2,1)}, bf16[256,384]{1,0:T(8,128)(2,1)S(1)}, u32[]{:S(2)}) copy-start(bf16[256,384]{1,0:T(8,128)(2,1)S(1)} %get-tuple-element.91.value) | copy-start | bytes 589828
  106.8 9.6 %copy-start.31 = (s32[12]{0:T(128)}, s32[12]{0:T(128)S(1)}, u32[]{:S(2)}) copy-start(s32[12]{0:T(128)S(1)} %or_convert_fusion.live) | copy-start | bytes 148
  106.8 9.6 %copy-start.10 = (s32[256,1]{1,0:T(8,128)}, s32[256,1]{1,0:T(8,128)S(1)}, u32[]{:S(2)}) copy-start(s32[256,1]{1,0:T(8,128)S(1)} %bitcast_select_fusion.self_id) | copy-start | bytes 3076
  327.1 5.7 %copy-start.43 = (f32[1,192]{1,0:T(1,128)S(1)}, f32[1,192]{1,0:T(1,128)}, u32[]{:S(2)}) copy-start(f32[1,192]{1,0:T(1,128)} %get-tuple-element.140) | copy-start | bytes 2308
  327.1 6.3 %copy-start.42 = (f32[1,192]{1,0:T(1,128)S(1)}, f32[1,192]{1,0:T(1,128)}, u32[]{:S(2)}) copy-start(f32[1,192]{1,0:T(1,128)} %get-tuple-element.141) | copy-start | bytes 2308
  327.1 6.8 %copy-start.41 = (f32[8,6]{1,0:T(8,128)S(1)}, f32[8,6]{1,0:T(8,128)}, u32[]{:S(2)}) copy-start(f32[8,6]{1,0:T(8,128)} %get-tuple-element.207) | copy-start | bytes 580
  327.1 7.4 %copy-start.40 = (f32[8,6]{1,0:T(8,128)S(1)}, f32[8,6]{1,0:T(8,128)}, u32[]{:S(2)}) copy-start(f32[8,6]{1,0:T(8,128)} %get-tuple-element.208) | copy-start | bytes 580
  327.1 8.0 %copy-start.39 = (f32[8,6]{1,0:T(8,128)S(1)}, f32[8,6]{1,0:T(8,128)}, u32[]{:S(2)}) copy-start(f32[8,6]{1,0:T(8,128)} %get-tuple-element.209) | copy-start | bytes 580
  327.1 8.6 %copy-start.46 = (f32[1,6]{1,0:T(1,128)S(1)}, f32[1,6]{1,0:T(1,128)}, u32[]{:S(2)}) copy-start(f32[1,6]{1,0:T(1,128)} %get-tuple-element.145) | copy-start | bytes 76
  (16 other events, 42.8 us)
Sparse Core Ops, SparseCore 0:
  86.5 58.5 all-gather.1
